TPU v7x, 256 devices: a whole 4x4x8 slice. The times are simulated.
256 devices in a mesh: shot: 8 (over x, z_hi), slab: 32 (over z_lo, y, core).
Axes of the slice: x: 4, y: 4, z: 8 (z_hi: 2, z_lo: 4; z = z_hi * 4 + z_lo), core: 2. Of those that a mesh axis runs over, the one named last changes fastest.
Arguments:
- fwd_last: float32 [8, 512, 64, 128], P('shot', 'slab'), may hold values from -6 to 6
- fwd_prev: float32 [8, 512, 64, 128], P('shot', 'slab'), may hold values from -6 to 6
- velocity: float32 [512, 64, 128], P('slab'), may hold values from 0.5 to 1
- aperture: int32 [8, 64, 128], P('shot'), may hold values 0 or 1
- rec_index: int32 [8, 2048], P('shot'), may hold values from 0 to 4194303
- src_index: int32 [8], P('shot'), may hold values from 0 to 4194303
- residual: float32 [8, 32, 2048], P('shot'), may hold values from -6 to 6
Outputs:
- gradient: float32 [512, 64, 128], P('slab', 'shot')
- adjoint_field: float32 [8, 512, 64, 128], P('shot', 'slab')
All inputs are finite; a program needn't handle non-finite values. No bound on the sum of `aperture` on one device may be relied on, other than what follows from the above.
Results may differ from a plain program's by a relative error of at most 0.000025.
Values sent between devices are 32-bit elements; how exact they have to be, the bound alone decides.
A program may use at most 256 MiB of HBM per device.

v0:
```python
import jax
import jax.numpy as jnp
from jax import lax
from jax.sharding import PartitionSpec as P

COEFS = (-205.0 / 72.0, 8.0 / 5.0, -1.0 / 5.0, 8.0 / 315.0, -1.0 / 560.0)
BLOCK_STEPS = 8


def with_halo(array, sides, width):
    for axis, dim in sides:
        count, length = (lax.axis_size(axis), array.shape[dim])
        up = [(i, (i + 1) % count) for i in range(count - 1)]
        down = [(j, i) for i, j in up]
        last = lax.slice_in_dim(array, length - width, length, axis=dim)
        initial = lax.slice_in_dim(array, 0, width, axis=dim)
        before = lax.ppermute(last, axis, up)
        after = lax.ppermute(initial, axis, down)
        array = jnp.concatenate([before, array, after], axis=dim)
    return array


def second_diff(padded, lower, count):
    centre = padded[:, lower : lower + count]
    total = 3.0 * COEFS[0] * centre
    for k in range(1, 5):
        total = total + COEFS[k] * (
            padded[:, lower + k : lower + k + count] + padded[:, lower - k : lower - k + count]
        )
    width_x = centre.shape[2]
    width_y = centre.shape[3]
    sides = jnp.pad(centre, ((0, 0), (0, 0), (4, 4), (4, 4)))
    for k in range(1, 5):
        total = total + COEFS[k] * (
            sides[:, :, 4 + k : 4 + k + width_x, 4 : 4 + width_y]
            + sides[:, :, 4 - k : 4 - k + width_x, 4 : 4 + width_y]
        )
    for k in range(1, 5):
        total = total + COEFS[k] * (
            sides[:, :, 4 : 4 + width_x, 4 + k : 4 + k + width_y]
            + sides[:, :, 4 : 4 + width_x, 4 - k : 4 - k + width_y]
        )
    return total


def ricker(step):
    arg = (jnp.pi * 0.06 * (step - 10.0)) ** 2
    return 10.0 * (1.0 - 2.0 * arg) * jnp.exp(-arg)


def on_device(fwd_last, fwd_prev, velocity, aperture, rec_index, src_index, residual):
    shots, depth, width_x, width_y = fwd_last.shape
    total_steps = residual.shape[1]
    plane = width_x * width_y
    ext_layers = depth + 8
    start_cell = lax.axis_index("slab") * depth * plane
    ext_base = start_cell - 4 * plane
    coef = (0.4 * velocity) ** 2
    gate_f = aperture.astype(jnp.float32)[:, None]
    cell_ids = jnp.arange(ext_layers * plane, dtype=jnp.int32)
    src_local = src_index - ext_base
    rec_local = rec_index - ext_base
    rec_valid = (rec_local >= 0) & (rec_local < ext_layers * plane)
    rec_local = jnp.where(rec_valid, rec_local, 0)
    shot_rows = jnp.broadcast_to(jnp.arange(shots, dtype=jnp.int32)[:, None], rec_local.shape)

    def rec_table(lowest):
        traces = lax.dynamic_slice_in_dim(residual, lowest, BLOCK_STEPS, 1)
        values = jnp.where(rec_valid[:, :, None], jnp.transpose(traces, (0, 2, 1)), 0.0)
        table = (
            jnp.zeros((shots, ext_layers * plane, BLOCK_STEPS), jnp.float32)
            .at[shot_rows, rec_local]
            .add(values)
        )
        return jnp.transpose(table, (0, 2, 1))

    def sources(step, table, lowest):
        wave = ricker(step.astype(jnp.float32))
        u_part = jnp.where(cell_ids[None, :] == src_local[:, None], wave, 0.0)
        l_part = lax.dynamic_index_in_dim(table, step - lowest, 1, keepdims=False)
        both = jnp.concatenate([u_part, l_part], axis=0).reshape(
            2 * shots, ext_layers, width_x, width_y
        )
        return both[:, 4 : 4 + depth]

    def term(u_cur, l_next, l_cur, l_new):
        return jnp.sum(gate_f * u_cur * (l_next - 2.0 * l_cur + l_new), axis=0)

    def block_run(b, carry):
        lowest = total_steps - BLOCK_STEPS - BLOCK_STEPS * b
        table = rec_table(lowest)

        def one_step(k, carry):
            nxt, cur, acc = carry
            step = total_steps - 1 - k
            padded = with_halo(cur, (("slab", 1),), 4)
            lap_now = second_diff(padded, 4, depth)
            fresh = 2.0 * cur - nxt + coef * (lap_now + sources(step, table, lowest))
            acc = acc + term(cur[:shots], nxt[shots:], cur[shots:], fresh[shots:])
            return (cur, fresh, acc)

        return lax.fori_loop(BLOCK_STEPS * b, BLOCK_STEPS * b + BLOCK_STEPS, one_step, carry)

    zero_l = jnp.zeros_like(fwd_last)
    nxt0 = jnp.concatenate([fwd_last, zero_l], axis=0)
    cur0 = jnp.concatenate([fwd_prev, zero_l], axis=0)
    zero_g = jnp.zeros((depth, width_x, width_y), jnp.float32)
    final = lax.fori_loop(
        0 // BLOCK_STEPS, total_steps // BLOCK_STEPS, block_run, (nxt0, cur0, zero_g)
    )
    summed = lax.psum_scatter(final[2], "shot", scatter_dimension=1, tiled=True)
    block = width_x // lax.axis_size("shot")
    speed_blk = lax.dynamic_slice_in_dim(velocity, lax.axis_index("shot") * block, block, 1)
    gradient = -2.0 / speed_blk * summed
    adjoint_field = final[1][shots:]
    return (gradient, adjoint_field)


def solution(mesh):
    in_specs = (
        P("shot", "slab", None, None),
        P("shot", "slab", None, None),
        P("slab", None, None),
        P("shot", None, None),
        P("shot", None),
        P("shot"),
        P("shot", None, None),
    )
    out_specs = (P("slab", "shot", None), P("shot", "slab", None, None))
    return jax.shard_map(
        on_device, mesh=mesh, in_specs=in_specs, out_specs=out_specs, check_vma=False
    )
```

profile of v0, /device:TPU:32, one launch (start us, length us, event | category | flops | bytes accessed | tf_op | source)
XLA Modules:
  0.0 2093.9 jit_solution(18077017737200803555)
XLA Ops:
  13.4 1985.2 %while.62 = (s32[]{:T(128)}, f32[2,16,64,128]{3,2,1,0:T(8,128)}, f32[2,16,64,128]{3,2,1,0:T(8,128)S(1)}, f32[16,64,128]{2,1,0:T(8,128)}, s32[1,2048]{1,0:T(1,128...) while((s32[]{:T(128)}, f32[2,16,64,128]{3,2,1,0:T(8,128)}, ...), condition=%wide.region_4.5_spmd.clone, body=%wide.region_0.4_spmd.clone.sunk | while | flops 12513304 | bytes 62303260 | solution.py:108
  15.2 31.1 %broadcast.247 = f32[196608,8]{1,0:T(8,128)} broadcast(f32[]{:T(128)} %constant.235.clone.1..sunk), dimensions={} | broadcast | bytes 6291460 | tf_op jit(solution)/shard_map/while
  46.3 264.9 %scatter_fusion = f32[196608,8]{1,0:T(8,128)} fusion(f32[196608,8]{1,0:T(8,128)} %broadcast.247, s32[2048]{0:T(1024)S(1)} %broadcast_select_fusion.2, f32[2048,8]{1,0:T(8,128)S(1)} %select_bitcast_fusion.2), kind=kCustom, calls=%fused_computation.clone.clone.1 | custom fusion | flops 16384 | bytes 204800 | tf_op jit(solution)/shard_map/while
  311.3 50.7 %copy.17 = f32[1,8,196608]{2,1,0:T(8,128)} copy(f32[1,8,196608]{1,2,0:T(8,128)} %bitcast.30) | data formatting | bytes 12582912 | tf_op jit(solution)/shard_map/while/body/eval_jaxpr/while | solution.py:102
  362.0 147.6 %while.63 = (s32[]{:T(128)}, f32[2,16,64,128]{3,2,1,0:T(8,128)}, f32[2,16,64,128]{3,2,1,0:T(8,128)S(1)}, f32[16,64,128]{2,1,0:T(8,128)}, s32[]{:T(128)}, /*index...) while((s32[]{:T(128)}, f32[2,16,64,128]{3,2,1,0:T(8,128)}, ...), condition=%wide.region_3.3_spmd, body=%wide.region_2.2_spmd.sunk | while | flops 12451856 | bytes 41976360 | solution.py:102
  365.2 5.3 collective-permute-start.1
  370.6 3.1 constant_dynamic-slice_fusion.5
  383.2 5.8 collective-permute-start.1
  389.1 3.1 constant_dynamic-slice_fusion.5
  401.7 5.8 collective-permute-start.1
  407.5 3.1 constant_dynamic-slice_fusion.5
  420.1 5.8 collective-permute-start.1
  426.0 3.1 constant_dynamic-slice_fusion.5
  438.6 5.8 collective-permute-start.1
  444.4 3.1 constant_dynamic-slice_fusion.5
  457.0 5.8 collective-permute-start.1
  462.9 3.1 constant_dynamic-slice_fusion.5
  475.5 5.8 collective-permute-start.1
  481.3 3.1 constant_dynamic-slice_fusion.5
  493.9 5.8 collective-permute-start.1
  499.8 3.1 constant_dynamic-slice_fusion.5
  511.5 31.1 %broadcast.247 = f32[196608,8]{1,0:T(8,128)} broadcast(f32[]{:T(128)} %constant.235.clone.1..sunk), dimensions={} | broadcast | bytes 6291460 | tf_op jit(solution)/shard_map/while
  542.6 264.9 %scatter_fusion = f32[196608,8]{1,0:T(8,128)} fusion(f32[196608,8]{1,0:T(8,128)} %broadcast.247, s32[2048]{0:T(1024)S(1)} %broadcast_select_fusion.2, f32[2048,8]{1,0:T(8,128)S(1)} %select_bitcast_fusion.2), kind=kCustom, calls=%fused_computation.clone.clone.1 | custom fusion | flops 16384 | bytes 204800 | tf_op jit(solution)/shard_map/while
  807.5 50.7 %copy.17 = f32[1,8,196608]{2,1,0:T(8,128)} copy(f32[1,8,196608]{1,2,0:T(8,128)} %bitcast.30) | data formatting | bytes 12582912 | tf_op jit(solution)/shard_map/while/body/eval_jaxpr/while | solution.py:102
  858.3 147.7 %while.63 = (s32[]{:T(128)}, f32[2,16,64,128]{3,2,1,0:T(8,128)}, f32[2,16,64,128]{3,2,1,0:T(8,128)S(1)}, f32[16,64,128]{2,1,0:T(8,128)}, s32[]{:T(128)}, /*index...) while((s32[]{:T(128)}, f32[2,16,64,128]{3,2,1,0:T(8,128)}, ...), condition=%wide.region_3.3_spmd, body=%wide.region_2.2_spmd.sunk | while | flops 12451856 | bytes 41976360 | solution.py:102
  861.0 5.9 collective-permute-start.1
  867.0 3.1 constant_dynamic-slice_fusion.5
  879.6 5.8 collective-permute-start.1
  885.4 3.1 constant_dynamic-slice_fusion.5
  898.0 5.8 collective-permute-start.1
  916.5 5.8 collective-permute-start.1
  934.9 5.8 collective-permute-start.1
  940.8 3.1 constant_dynamic-slice_fusion.5
  953.4 5.8 collective-permute-start.1
  971.8 5.8 collective-permute-start.1
  990.3 5.8 collective-permute-start.1
  996.1 3.1 constant_dynamic-slice_fusion.5
  1007.8 31.1 %broadcast.247 = f32[196608,8]{1,0:T(8,128)} broadcast(f32[]{:T(128)} %constant.235.clone.1..sunk), dimensions={} | broadcast | bytes 6291460 | tf_op jit(solution)/shard_map/while
  1038.9 264.9 %scatter_fusion = f32[196608,8]{1,0:T(8,128)} fusion(f32[196608,8]{1,0:T(8,128)} %broadcast.247, s32[2048]{0:T(1024)S(1)} %broadcast_select_fusion.2, f32[2048,8]{1,0:T(8,128)S(1)} %select_bitcast_fusion.2), kind=kCustom, calls=%fused_computation.clone.clone.1 | custom fusion | flops 16384 | bytes 204800 | tf_op jit(solution)/shard_map/while
  1303.8 50.7 %copy.17 = f32[1,8,196608]{2,1,0:T(8,128)} copy(f32[1,8,196608]{1,2,0:T(8,128)} %bitcast.30) | data formatting | bytes 12582912 | tf_op jit(solution)/shard_map/while/body/eval_jaxpr/while | solution.py:102
  1354.6 147.7 %while.63 = (s32[]{:T(128)}, f32[2,16,64,128]{3,2,1,0:T(8,128)}, f32[2,16,64,128]{3,2,1,0:T(8,128)S(1)}, f32[16,64,128]{2,1,0:T(8,128)}, s32[]{:T(128)}, /*index...) while((s32[]{:T(128)}, f32[2,16,64,128]{3,2,1,0:T(8,128)}, ...), condition=%wide.region_3.3_spmd, body=%wide.region_2.2_spmd.sunk | while | flops 12451856 | bytes 41976360 | solution.py:102
  1357.4 5.9 collective-permute-start.1
  1363.3 3.1 constant_dynamic-slice_fusion.5
  1375.9 5.8 collective-permute-start.1
  1394.4 5.8 collective-permute-start.1
  1412.8 5.8 collective-permute-start.1
  1418.6 3.1 constant_dynamic-slice_fusion.5
  1431.3 5.8 collective-permute-start.1
  1449.7 5.8 collective-permute-start.1
  1468.2 5.8 collective-permute-start.1
  1486.6 5.8 collective-permute-start.1
  1504.1 31.1 %broadcast.247 = f32[196608,8]{1,0:T(8,128)} broadcast(f32[]{:T(128)} %constant.235.clone.1..sunk), dimensions={} | broadcast | bytes 6291460 | tf_op jit(solution)/shard_map/while
  1535.2 264.9 %scatter_fusion = f32[196608,8]{1,0:T(8,128)} fusion(f32[196608,8]{1,0:T(8,128)} %broadcast.247, s32[2048]{0:T(1024)S(1)} %broadcast_select_fusion.2, f32[2048,8]{1,0:T(8,128)S(1)} %select_bitcast_fusion.2), kind=kCustom, calls=%fused_computation.clone.clone.1 | custom fusion | flops 16384 | bytes 204800 | tf_op jit(solution)/shard_map/while
  1800.2 50.7 %copy.17 = f32[1,8,196608]{2,1,0:T(8,128)} copy(f32[1,8,196608]{1,2,0:T(8,128)} %bitcast.30) | data formatting | bytes 12582912 | tf_op jit(solution)/shard_map/while/body/eval_jaxpr/while | solution.py:102
  1850.9 147.7 %while.63 = (s32[]{:T(128)}, f32[2,16,64,128]{3,2,1,0:T(8,128)}, f32[2,16,64,128]{3,2,1,0:T(8,128)S(1)}, f32[16,64,128]{2,1,0:T(8,128)}, s32[]{:T(128)}, /*index...) while((s32[]{:T(128)}, f32[2,16,64,128]{3,2,1,0:T(8,128)}, ...), condition=%wide.region_3.3_spmd, body=%wide.region_2.2_spmd.sunk | while | flops 12451856 | bytes 41976360 | solution.py:102
  1853.7 5.9 collective-permute-start.1
  1872.3 5.8 collective-permute-start.1
  1890.7 5.8 collective-permute-start.1
  1909.2 5.8 collective-permute-start.1
  1927.6 5.8 collective-permute-start.1
  1946.1 5.8 collective-permute-start.1
  1964.5 5.8 collective-permute-start.1
  1983.0 5.8 collective-permute-start.1
  1999.5 86.0 %reduce-scatter.2.cloned.1.call-done = f32[16,8,128]{2,1,0:T(8,128)} async-done(((f32[16,64,128]{2,1,0:T(8,128)}), f32[16,8,128]{2,1,0:T(8,128)}) %reduce-scatter.2.cloned.1.call-update) | async-done | bytes 65552 | tf_op jit(solution)/shard_map/reduce_scatter | solution.py:111
  (715 shorter events, 371.1 us)
Async XLA Ops:
  7.2 2078.4 %reduce-scatter.2.cloned.1.call-start = ((), (), s32[]{:S(2)}) async-start(), calls=%async_computation.1 | async-start | bytes 589824 | tf_op jit(solution)/shard_map/reduce_scatter | solution.py:111
  362.9 11.0 collective-permute-start
  381.3 11.0 collective-permute-start
  383.2 10.3 collective-permute-start.1
  399.8 11.0 collective-permute-start
  401.7 10.3 collective-permute-start.1
  418.2 11.0 collective-permute-start
  420.1 10.3 collective-permute-start.1
  436.7 11.0 collective-permute-start
  438.6 10.3 collective-permute-start.1
  455.1 11.0 collective-permute-start
  457.0 10.3 collective-permute-start.1
  473.6 11.0 collective-permute-start
  475.5 10.3 collective-permute-start.1
  492.0 11.0 collective-permute-start
  493.9 10.3 collective-permute-start.1
  859.1 11.1 collective-permute-start
  861.0 10.4 collective-permute-start.1
  877.7 11.0 collective-permute-start
  879.6 10.3 collective-permute-start.1
  896.1 11.0 collective-permute-start
  898.0 10.3 collective-permute-start.1
  914.6 11.0 collective-permute-start
  916.5 10.3 collective-permute-start.1
  933.0 11.0 collective-permute-start
  934.9 10.3 collective-permute-start.1
  951.5 11.0 collective-permute-start
  953.4 10.3 collective-permute-start.1
  969.9 11.0 collective-permute-start
  971.8 10.3 collective-permute-start.1
  988.4 11.0 collective-permute-start
  990.3 10.3 collective-permute-start.1
  1355.5 11.1 collective-permute-start
  1357.4 10.4 collective-permute-start.1
  1374.0 11.0 collective-permute-start
  1375.9 10.3 collective-permute-start.1
  1392.5 11.0 collective-permute-start
  1394.4 10.3 collective-permute-start.1
  1410.9 11.0 collective-permute-start
  1412.8 10.3 collective-permute-start.1
  1429.4 11.0 collective-permute-start
  1431.3 10.3 collective-permute-start.1
  1447.8 11.0 collective-permute-start
  1449.7 10.3 collective-permute-start.1
  1466.3 11.0 collective-permute-start
  1468.2 10.3 collective-permute-start.1
  1484.7 11.0 collective-permute-start
  1486.6 10.3 collective-permute-start.1
  1851.8 11.1 collective-permute-start
  1853.7 10.4 collective-permute-start.1
  1870.3 11.0 collective-permute-start
  1872.3 10.3 collective-permute-start.1
  1888.8 11.0 collective-permute-start
  1890.7 10.3 collective-permute-start.1
  1907.2 11.0 collective-permute-start
  1909.2 10.3 collective-permute-start.1
  1925.7 11.0 collective-permute-start
  1927.6 10.3 collective-permute-start.1
  1944.1 11.0 collective-permute-start
  1946.1 10.3 collective-permute-start.1
  1962.6 11.0 collective-permute-start
  1964.5 10.3 collective-permute-start.1
  1981.0 11.0 collective-permute-start
  1983.0 10.3 collective-permute-start.1
  (134 other events, 234.3 us)
Sparse Core Ops, SparseCore 0:
  1998.8 86.6 reduce-scatter.1
where the time goes:
time: 2130 us; the launch traced here: 2090 us
  other arithmetic  1170 us (55%)
  local copies, waits for them, and re-layouts  575 us (27%)
  starting transfers between devices  246 us (12%)
  waiting for transfers between devices  86.2 us (4%)
    while x16, other arithmetic  1060 us
    while x4, local copies, waits for them, and re-layouts, block_run(): lax.fori_loop(BLOCK_STEPS * b, BLOCK_STEPS * b + BLOCK_STEPS, one_step, c...  203 us
    while x388, local copies, waits for them, and re-layouts  201 us
    ppermute x32, starting transfers between devices, with_halo(): after = lax.ppermute(initial, axis, down)  184 us
    dynamic_slice x32, local copies, waits for them, and re-layouts, sources(): l_part = lax.dynamic_index_in_dim(table, step - lowest, 1, keepdims=False)  101 us
    reduce_scatter x1, waiting for transfers between devices, on_device(): summed = lax.psum_scatter(final[2], 'shot', scatter_dimension=1, tiled=True)  86 us
    add x32, other arithmetic, one_step(): fresh = 2.0 * cur - nxt + coef * (lap_now + sources(step, table, lowest))  86 us
    ppermute x32, starting transfers between devices, with_halo(): before = lax.ppermute(last, axis, up)  61.5 us
  transfers between devices with their start and end apart: 65, of which 1 were waited for; matrix products, arithmetic and copies ran while one was open for 7% of the time, Pallas kernels for 0%

commit v1 on v0

v1 whole, which is shorter than its diff:
```python
import functools

import jax
import jax.numpy as jnp
import numpy as np
from jax import lax
from jax.experimental import pallas as pl
from jax.experimental.pallas import tpu as pltpu
from jax.sharding import PartitionSpec as P

SCALE = 5040.0
CENTRE = -43050.0
WEIGHTS = (8064.0, -1008.0, 128.0, -9.0)
HALO = 4
MESH = pl.DeviceIdType.MESH


def ricker(step):
    arg = (jnp.pi * 0.06 * (step - 10.0)) ** 2
    return 10.0 * (1.0 - 2.0 * arg) * jnp.exp(-arg)


def band(size):
    matrix = np.zeros((size, size), np.float32)
    for k, weight in enumerate(WEIGHTS, 1):
        matrix += weight * (np.eye(size, k=k) + np.eye(size, k=-k))
    return matrix


def table_kernel(chunk, rec_ref, res_ref, out_ref, table, picked):
    steps, lanes = res_ref.shape[1], table.shape[1]
    rows = table.shape[0] // steps
    receivers = rec_ref.shape[1]
    cells = rows * lanes
    base = lax.axis_index("slab") * cells
    part = pl.program_id(0)

    @pl.when(part == 0)
    def _():
        group = 8
        rows_each = rows // (receivers // group)

        def scan(i, count):
            for j in range(group):
                r = i * group + j
                local = rec_ref[0, r] - base
                picked[count] = r
                inside = jnp.logical_and(local >= 0, local < cells)
                count = count + inside.astype(jnp.int32)
            clear = pl.multiple_of(i * (rows_each * steps), rows_each * steps)
            table[pl.ds(clear, rows_each * steps)] = jnp.zeros((rows_each * steps, lanes), jnp.float32)
            return count

        count = lax.fori_loop(0, receivers // group, scan, jnp.int32(0))
        lane_ids = lax.broadcasted_iota(jnp.int32, (steps, lanes), 1)

        def add(i, carry):
            r = picked[i]
            local = rec_ref[0, r] - base
            row = local // lanes
            lane = local % lanes
            start = pl.multiple_of((r // lanes) * lanes, lanes)
            traces = res_ref[0, :, pl.ds(start, lanes)]
            moved = pltpu.roll(traces, (lane - r) & (lanes - 1), axis=1)
            place = pl.ds(pl.multiple_of(row * steps, steps), steps)
            table[place] = table[place] + jnp.where(lane_ids == lane, SCALE * moved, 0.0)
            return carry

        lax.fori_loop(0, count, add, 0)

    depth, wide = out_ref.shape[1:3]
    for c in range(chunk):
        n = part * chunk + c

        def layer(z, carry):
            out_ref[c, z] = table[pl.ds(z * wide * steps + n, wide, stride=steps), :]
            return carry

        lax.fori_loop(0, depth, layer, 0, unroll=4)


def receiver_table(rec_index, residual, depth, wide, lanes):
    steps = residual.shape[1]
    chunk = 4
    return pl.pallas_call(
        functools.partial(table_kernel, chunk),
        grid=(steps // chunk,),
        out_shape=jax.ShapeDtypeStruct((steps, depth, wide, lanes), jnp.float32),
        in_specs=[
            pl.BlockSpec(memory_space=pltpu.SMEM),
            pl.BlockSpec(residual.shape, lambda i: (0, 0, 0)),
        ],
        out_specs=pl.BlockSpec((chunk, depth, wide, lanes), lambda i: (i, 0, 0, 0)),
        scratch_shapes=[
            pltpu.VMEM((depth * wide * steps, lanes), jnp.float32),
            pltpu.SMEM((rec_index.shape[1],), jnp.int32),
        ],
        compiler_params=pltpu.CompilerParams(vmem_limit_bytes=32 * 1024 * 1024),
    )(rec_index, residual)


def adjoint_kernel(
    groups, last_ref, prev_ref, vel_ref, gate_ref, src_ref, wave_ref, rec_ref, mx_ref, my_ref,
    grad_ref, adj_ref,
    u_buf, l_buf, coef, src_coef, image, rec_buf, first, second, part_sum,
    u_send, u_recv, l_send, l_recv, rec_sem, io_sem, sum_send, sum_recv,
):
    depth, wide, lanes = last_ref.shape[1:]
    steps = rec_ref.shape[0]
    n_x, n_hi = groups
    shot = lax.axis_index("shot")
    slab = lax.axis_index("slab")
    slabs = lax.axis_size("slab")
    x, hi = shot // n_hi, shot % n_hi
    top = depth + HALO

    load_prev = pltpu.make_async_copy(prev_ref.at[0], u_buf.at[0, pl.ds(HALO, depth)], io_sem.at[0])
    load_last = pltpu.make_async_copy(last_ref.at[0], u_buf.at[1, pl.ds(HALO, depth)], io_sem.at[1])
    load_prev.start()
    load_last.start()

    def load_rec(s):
        slot = lax.rem(s, 2)
        return pltpu.make_async_copy(rec_ref.at[steps - 1 - s], rec_buf.at[slot], rec_sem.at[slot])

    load_rec(0).start()

    empty = jnp.zeros((HALO, wide, lanes), jnp.float32)
    for q in range(2):
        u_buf[q, 0:HALO] = empty
        u_buf[q, top : top + HALO] = empty
        for z in range(0, depth + 2 * HALO, HALO):
            l_buf[q, z : z + HALO] = empty

    barrier = pltpu.get_barrier_semaphore()
    peers = [(lax.rem(x + d, n_x) * n_hi + hi, slab) for d in range(1, n_x)]
    peers += [(x * n_hi + lax.rem(hi + d, n_hi), slab) for d in range(1, n_hi)]
    for peer in peers:
        pl.semaphore_signal(barrier, inc=1, device_id=peer, device_id_type=MESH)

    @pl.when(slab > 0)
    def _():
        pl.semaphore_signal(barrier, inc=1, device_id=(shot, slab - 1), device_id_type=MESH)

    @pl.when(slab < slabs - 1)
    def _():
        pl.semaphore_signal(barrier, inc=1, device_id=(shot, slab + 1), device_id_type=MESH)

    ends = (slab > 0).astype(jnp.int32) + (slab < slabs - 1).astype(jnp.int32)
    pl.semaphore_wait(barrier, len(peers) + ends)

    def down_copy(buf, send, recv, q, source=None):
        return pltpu.make_async_remote_copy(
            src_ref=buf.at[q, pl.ds(HALO, HALO)] if source is None else source,
            dst_ref=buf.at[q, pl.ds(top, HALO)],
            send_sem=send.at[q, 0],
            recv_sem=recv.at[q, 1],
            device_id=(shot, slab - 1),
            device_id_type=MESH,
        )

    def up_copy(buf, send, recv, q, source=None):
        return pltpu.make_async_remote_copy(
            src_ref=buf.at[q, pl.ds(depth, HALO)] if source is None else source,
            dst_ref=buf.at[q, pl.ds(0, HALO)],
            send_sem=send.at[q, 1],
            recv_sem=recv.at[q, 0],
            device_id=(shot, slab + 1),
            device_id_type=MESH,
        )

    @pl.when(slab > 0)
    def _():
        down_copy(u_buf, u_send, u_recv, 0, prev_ref.at[0, pl.ds(0, HALO)]).start()

    @pl.when(slab < slabs - 1)
    def _():
        up_copy(u_buf, u_send, u_recv, 0, prev_ref.at[0, pl.ds(depth - HALO, HALO)]).start()

    ids = lax.broadcasted_iota(jnp.int32, (wide, lanes), 0) * lanes + lax.broadcasted_iota(
        jnp.int32, (wide, lanes), 1
    )
    source = src_ref[0] - slab * (depth * wide * lanes)

    def prepare(z, carry):
        speed = 0.4 * vel_ref[z]
        value = speed * speed
        coef[z] = value * (1.0 / SCALE)
        src_coef[z] = jnp.where(ids == source - z * (wide * lanes), value, 0.0)
        image[:, z] = jnp.zeros((wide // 8, 8, lanes), jnp.float32)
        return carry

    lax.fori_loop(0, depth, prepare, 0)
    load_prev.wait()
    load_last.wait()

    def laplace(buf, q, z):
        f = buf[q, z + HALO]
        hi_part = f.astype(jnp.bfloat16)
        rest = f - hi_part.astype(jnp.float32)
        mid_part = rest.astype(jnp.bfloat16)
        lo_part = (rest - mid_part.astype(jnp.float32)).astype(jnp.bfloat16)
        total = CENTRE * f
        for k, weight in enumerate(WEIGHTS, 1):
            total = total + weight * (buf[q, z + HALO + k] + buf[q, z + HALO - k])
        total = total + jnp.dot(
            mx_ref[...],
            jnp.concatenate([hi_part, mid_part, lo_part], axis=0),
            preferred_element_type=jnp.float32,
        )
        total = total + jnp.dot(
            jnp.concatenate([hi_part, mid_part, lo_part], axis=1),
            my_ref[...],
            preferred_element_type=jnp.float32,
        )
        return f, total

    def u_layers(s, q, first_layer):
        wave = wave_ref[s]
        for z in range(first_layer, first_layer + HALO):
            f, lap = laplace(u_buf, q, z)
            u_buf[1 - q, z + HALO] = (
                2.0 * f - u_buf[1 - q, z + HALO] + coef[z] * lap + wave * src_coef[z]
            )

    def l_layers(s, q, first_layer):
        for z in range(first_layer, first_layer + HALO):
            f, lap = laplace(l_buf, q, z)
            forced = lap + rec_buf[q, z]
            l_buf[1 - q, z + HALO] = 2.0 * f - l_buf[1 - q, z + HALO] + coef[z] * forced
            term = u_buf[q, z + HALO] * forced
            image[:, z] = image[:, z] + term.reshape(wide // 8, 8, lanes)

    has_down, has_up = slab > 0, slab < slabs - 1

    def advance(s, q, buf, send, recv, layers, can_recv, can_wait_send, can_send):
        def both(a, b):
            return a if b is True else jnp.logical_and(a, b)

        for has, copy, edge in ((has_down, down_copy, 0), (has_up, up_copy, 1)):
            @pl.when(both(has, can_recv))
            def _():
                (up_copy if edge == 0 else down_copy)(buf, send, recv, q).wait_recv()

            @pl.when(both(has, can_wait_send))
            def _():
                copy(buf, send, recv, 1 - q).wait_send()

            layers(s, q, 0 if edge == 0 else depth - HALO)

            if can_send is not False:
                @pl.when(both(has, can_send))
                def _():
                    copy(buf, send, recv, 1 - q).start()

        for z in range(HALO, depth - HALO, HALO):
            layers(s, q, z)

    def step(s, carry):
        q = lax.rem(s, 2)
        load_rec(s + 1).start()
        advance(s, q, u_buf, u_send, u_recv, u_layers, True, s >= 1, s < steps - 2)
        load_rec(s).wait()
        advance(s, q, l_buf, l_send, l_recv, l_layers, s >= 1, s >= 2, True)
        return carry

    lax.fori_loop(0, steps - 1, step, 0)
    s_end = steps - 1
    load_rec(s_end).wait()
    advance(s_end, s_end % 2, l_buf, l_send, l_recv, l_layers, True, True, False)

    store = pltpu.make_async_copy(
        l_buf.at[steps % 2, pl.ds(HALO, depth)], adj_ref.at[0], io_sem.at[0]
    )
    store.start()

    for b in range(wide // 8):
        gate = gate_ref[0, 8 * b : 8 * b + 8].astype(jnp.float32)
        image[b] = image[b] * gate

    copies = []
    for d in range(1, n_x):
        target = lax.rem(x + d, n_x)
        copies.append(
            pltpu.make_async_remote_copy(
                src_ref=image.at[pl.ds(target * n_hi, n_hi)],
                dst_ref=first.at[d - 1],
                send_sem=sum_send.at[d - 1],
                recv_sem=sum_recv.at[d - 1],
                device_id=(target * n_hi + hi, slab),
                device_id_type=MESH,
            )
        )
        copies[-1].start()
    for copy in copies:
        copy.wait_recv()
    for h in range(n_hi):
        total = image[x * n_hi + h]
        for d in range(1, n_x):
            total = total + first[d - 1, h]
        part_sum[h] = total
    for d in range(1, n_hi):
        target = lax.rem(hi + d, n_hi)
        copies.append(
            pltpu.make_async_remote_copy(
                src_ref=part_sum.at[target],
                dst_ref=second.at[d - 1],
                send_sem=sum_send.at[n_x - 2 + d],
                recv_sem=sum_recv.at[n_x - 2 + d],
                device_id=(x * n_hi + target, slab),
                device_id_type=MESH,
            )
        )
        copies[-1].start()
        copies[-1].wait_recv()
    total = part_sum[hi]
    for d in range(1, n_hi):
        total = total + second[d - 1]
    speed = vel_ref[:, pl.ds(pl.multiple_of(shot * 8, 8), 8), :]
    grad_ref[...] = (-0.32 / SCALE) * speed * total
    for copy in copies:
        copy.wait_send()
    store.wait()

    for buf, send, recv, q in (
        (u_buf, u_send, u_recv, (steps - 2) % 2),
        (l_buf, l_send, l_recv, (steps - 1) % 2),
    ):
        @pl.when(has_down)
        def _():
            down_copy(buf, send, recv, q).wait_send()

        @pl.when(has_up)
        def _():
            up_copy(buf, send, recv, q).wait_send()


def on_device(groups, fwd_last, fwd_prev, velocity, aperture, rec_index, src_index, residual):
    depth, wide, lanes = fwd_last.shape[1:]
    steps = residual.shape[1]
    n_x, n_hi = groups
    blocks = wide // 8
    table = receiver_table(rec_index, residual, depth, wide, lanes)
    waves = ricker((steps - 1 - jnp.arange(steps, dtype=jnp.int32)).astype(jnp.float32))
    mx = jnp.asarray(np.tile(band(wide), (1, 3)), jnp.bfloat16)
    my = jnp.asarray(np.tile(band(lanes), (3, 1)), jnp.bfloat16)
    hbm = pl.BlockSpec(memory_space=pl.ANY)
    vmem = pl.BlockSpec(memory_space=pltpu.VMEM)
    smem = pl.BlockSpec(memory_space=pltpu.SMEM)
    field = pltpu.VMEM((2, depth + 2 * HALO, wide, lanes), jnp.float32)
    grid = pltpu.VMEM((depth, wide, lanes), jnp.float32)
    pair = pltpu.SemaphoreType.DMA((2, 2))
    return pl.pallas_call(
        functools.partial(adjoint_kernel, groups),
        out_shape=(
            jax.ShapeDtypeStruct((depth, 8, lanes), jnp.float32),
            jax.ShapeDtypeStruct(fwd_last.shape, jnp.float32),
        ),
        in_specs=[hbm, hbm, vmem, vmem, smem, smem, hbm, vmem, vmem],
        out_specs=(vmem, hbm),
        scratch_shapes=[
            field, field, grid, grid,
            pltpu.VMEM((blocks, depth, 8, lanes), jnp.float32),
            pltpu.VMEM((2, depth, wide, lanes), jnp.float32),
            pltpu.VMEM((n_x - 1, n_hi, depth, 8, lanes), jnp.float32),
            pltpu.VMEM((n_hi - 1, depth, 8, lanes), jnp.float32),
            pltpu.VMEM((n_hi, depth, 8, lanes), jnp.float32),
            pair, pair, pair, pair,
            pltpu.SemaphoreType.DMA((2,)),
            pltpu.SemaphoreType.DMA((2,)),
            pltpu.SemaphoreType.DMA((n_x + n_hi - 2,)),
            pltpu.SemaphoreType.DMA((n_x + n_hi - 2,)),
        ],
        compiler_params=pltpu.CompilerParams(
            collective_id=0, has_side_effects=True, vmem_limit_bytes=32 * 1024 * 1024
        ),
    )(fwd_last, fwd_prev, velocity, aperture, src_index, waves, table, mx, my)


def solution(mesh):
    in_specs = (
        P("shot", "slab", None, None),
        P("shot", "slab", None, None),
        P("slab", None, None),
        P("shot", None, None),
        P("shot", None),
        P("shot"),
        P("shot", None, None),
    )
    out_specs = (P("slab", "shot", None), P("shot", "slab", None, None))
    shots = mesh.shape["shot"]
    groups = (shots // 2, 2)
    return jax.shard_map(
        functools.partial(on_device, groups),
        mesh=mesh, in_specs=in_specs, out_specs=out_specs, check_vma=False,
    )
```

time: 2130 us -> 226 us (0.11); the launches traced: 2090 us -> 225 us
  other arithmetic: 1170 us -> 0.01 us
  local copies, waits for them, and re-layouts: 575 us -> 14.6 us
  starting transfers between devices: 246 us -> 0 us
  Pallas kernels: 0 us -> 209 us
  waiting for transfers between devices: 86.2 us -> 0 us
    while x16 -> x0, other arithmetic: 1060 us -> none
    while x392 -> x0, local copies, waits for them, and re-layouts: 403 us -> none  [the longest x4 203 us: block_run(): lax.fori_loop(BLOCK_STEPS * b, BLOCK_STEPS * b + BLOCK_STEPS, one_step, c...]
    ppermute x64 -> x0, starting transfers between devices: 245 us -> none  [the longest x32 184 us: with_halo(): after = lax.ppermute(initial, axis, down)]
    pallas_call x0 -> x2, Pallas kernels: none -> 209 us  [the longest x1 179 us: on_device(): pl.pallas_call(functools.partial(adjoint_kernel, groups), out_shape=(jax....]
    dynamic_slice x40 -> x0, local copies, waits for them, and re-layouts: 105 us -> none  [the longest x32 101 us: sources(): l_part = lax.dynamic_index_in_dim(table, step - lowest, 1, keepdims=False)]
    add x64 -> x0, other arithmetic: 97.3 us -> none  [the longest x32 86 us: one_step(): fresh = 2.0 * cur - nxt + coef * (lap_now + sources(step, table, lowest))]
    reduce_scatter x1 -> x0, waiting for transfers between devices: 86 us -> none  [on_device(): summed = lax.psum_scatter(final[2], 'shot', scatter_dimension=1, tiled=True)]
    concatenate x34 -> x0, local copies, waits for them, and re-layouts: 37.7 us -> none  [the longest x32 35.4 us: with_halo(): array = jnp.concatenate([before, array, after], axis=dim)]
  transfers between devices with their start and end apart: 65 -> 0, of which waited for: 1 -> 0; matrix products, arithmetic and copies ran while one was open for 7% -> 0% of each run, Pallas kernels for 0% -> 0%
where the time goes in v1:
time: 226 us; the launch traced here: 225 us
  Pallas kernels  209 us (92%)
  local copies, waits for them, and re-layouts  14.6 us (6%)
    pallas_call x1, Pallas kernels, on_device(): pl.pallas_call(functools.partial(adjoint_kernel, groups), out_shape=(jax....  179 us
    pallas_call x1, Pallas kernels, receiver_table(): pl.pallas_call(functools.partial(table_kernel, chunk), grid=(steps // chu...  30.7 us
    unnamed x22, local copies, waits for them, and re-layouts  14.6 us

profile of v1, /device:TPU:32, one launch (start us, length us, event | category | flops | bytes accessed | tf_op | source)
XLA Modules:
  0.0 225.3 jit_solution(22768786033902645)
XLA Ops:
  0.6 0.0 copy-start.4
  0.6 0.0 copy-start.3
  0.7 0.0 copy-start.2
  1.4 0.0 copy-start.5
  1.4 0.9 copy-done.5
  2.4 0.0 copy-start.9
  2.4 0.7 copy-done.9
  3.1 0.0 copy-start.6
  3.1 0.0 copy-start.7
  3.1 0.0 copy-start.8
  3.1 30.7 %shard_map.104.rec_ref = f32[32,16,64,128]{3,2,1,0:T(8,128)S(1)} custom-call(s32[1,2048]{1,0:T(1,128)S(1)} %copy-done.9, f32[1,32,2048]{2,1,0:T(8,128)S(1)} %copy-done.5), custom_call_target="tpu_custom_call" | custom-call | tf_op jit(solution)/shard_map/pallas_call | solution.py:85
  33.8 0.0 copy-start
  33.8 5.7 %copy-done = f32[32,16,64,128]{3,2,1,0:T(8,128)} copy-done((f32[32,16,64,128]{3,2,1,0:T(8,128)}, f32[32,16,64,128]{3,2,1,0:T(8,128)S(1)}, u32[]{:S(2)}) %copy-start) | copy-done | bytes 16777240
  39.5 0.0 copy-done.4
  39.6 0.0 copy-done.3
  39.6 0.0 copy-done.2
  39.6 0.0 copy-done.6
  39.6 0.0 copy-done.7
  39.6 0.0 copy-done.8
  39.6 0.0 copy-start.1
  39.6 5.8 %copy-done.1 = f32[32,16,64,128]{3,2,1,0:T(8,128)S(1)} copy-done((f32[32,16,64,128]{3,2,1,0:T(8,128)S(1)}, f32[32,16,64,128]{3,2,1,0:T(8,128)}, u32[]{:S(2)}) %copy-start.1) | copy-done | bytes 16777240
  45.4 178.5 %shard_map.105 = (f32[16,8,128]{2,1,0:T(8,128)S(1)}, f32[1,16,64,128]{3,2,1,0:T(8,128)S(1)}) custom-call(f32[1,16,64,128]{3,2,1,0:T(8,128)S(1)} %copy-done.2, f32[1,16,64,128]{3,2,1,0:T(8,128)S(1)} %copy-done.3, f32[16,64,128]{2,1,0:T(8,128)S(1)} %copy-done.4, s32[1,64,128]{2,1,0:T(8,128)S(1)} %copy-done.7, s32[1]{0:T(128)S(6)} %copy.13.src_ref, ...), custom_call_target="tpu_custom_call" | custom-call | tf_op jit(solution)/shard_map/pallas_call | solution.py:353
  223.9 0.6 copy.14
  224.5 0.8 copy.15
  (1 shorter events, 0.0 us)
Async XLA Ops:
  0.6 38.9 %copy-start.4 = (f32[16,64,128]{2,1,0:T(8,128)S(1)}, f32[16,64,128]{2,1,0:T(8,128)}, u32[]{:S(2)}) copy-start(f32[16,64,128]{2,1,0:T(8,128)} %vel_ref.1) | copy-start | bytes 1572868
  0.6 38.9 %copy-start.3 = (f32[1,16,64,128]{3,2,1,0:T(8,128)S(1)}, f32[1,16,64,128]{3,2,1,0:T(8,128)}, u32[]{:S(2)}) copy-start(f32[1,16,64,128]{3,2,1,0:T(8,128)} %prev_ref.1) | copy-start | bytes 1572868
  0.7 38.9 %copy-start.2 = (f32[1,16,64,128]{3,2,1,0:T(8,128)S(1)}, f32[1,16,64,128]{3,2,1,0:T(8,128)}, u32[]{:S(2)}) copy-start(f32[1,16,64,128]{3,2,1,0:T(8,128)} %last_ref.1) | copy-start | bytes 1572868
  1.4 1.0 copy-start.5
  2.4 0.7 copy-start.9
  3.1 36.5 %copy-start.6 = (bf16[384,128]{1,0:T(8,128)(2,1)S(1)}, bf16[384,128]{1,0:T(8,128)(2,1)}, u32[]{:S(2)}) copy-start(bf16[384,128]{1,0:T(8,128)(2,1)} %constant.17.clone.my_ref) | copy-start | bytes 294916
  3.1 36.5 %copy-start.7 = (s32[1,64,128]{2,1,0:T(8,128)S(1)}, s32[1,64,128]{2,1,0:T(8,128)}, u32[]{:S(2)}) copy-start(s32[1,64,128]{2,1,0:T(8,128)} %gate_ref.1) | copy-start | bytes 98308
  3.1 36.5 %copy-start.8 = (bf16[64,192]{1,0:T(8,128)(2,1)S(1)}, bf16[64,192]{1,0:T(8,128)(2,1)}, u32[]{:S(2)}) copy-start(bf16[64,192]{1,0:T(8,128)(2,1)} %constant.16.clone.mx_ref) | copy-start | bytes 73732
  33.8 5.7 %copy-start = (f32[32,16,64,128]{3,2,1,0:T(8,128)}, f32[32,16,64,128]{3,2,1,0:T(8,128)S(1)}, u32[]{:S(2)}) copy-start(f32[32,16,64,128]{3,2,1,0:T(8,128)S(1)} %shard_map.104.rec_ref) | copy-start | bytes 50331652
  39.6 5.8 %copy-start.1 = (f32[32,16,64,128]{3,2,1,0:T(8,128)S(1)}, f32[32,16,64,128]{3,2,1,0:T(8,128)}, u32[]{:S(2)}) copy-start(f32[32,16,64,128]{3,2,1,0:T(8,128)} %copy-done) | copy-start | bytes 50331652

commit v2 on v1

v2 whole, which is shorter than its diff:
```python
import functools

import jax
import jax.numpy as jnp
import numpy as np
from jax import lax
from jax.experimental import pallas as pl
from jax.experimental.pallas import tpu as pltpu
from jax.sharding import PartitionSpec as P

SCALE = 5040.0
CENTRE = -43050.0
WEIGHTS = (8064.0, -1008.0, 128.0, -9.0)
HALO = 4
MESH = pl.DeviceIdType.MESH


def ricker(step):
    arg = (jnp.pi * 0.06 * (step - 10.0)) ** 2
    return 10.0 * (1.0 - 2.0 * arg) * jnp.exp(-arg)


def band(size):
    matrix = np.zeros((size, size), np.float32)
    for k, weight in enumerate(WEIGHTS, 1):
        matrix += weight * (np.eye(size, k=k) + np.eye(size, k=-k))
    return matrix


def table_kernel(first_row, rec_ref, res_ref, table, picked):
    steps, receivers = res_ref.shape[1:]
    lanes = table.shape[1]
    rows = table.shape[0] // steps
    cells = rows * lanes
    base = (lax.axis_index("slab") * (rows - 2 * first_row) - first_row) * lanes
    group = 8
    clear_rows = rows * steps // (receivers // group)

    def scan(i, count):
        for j in range(group):
            r = i * group + j
            local = rec_ref[0, r] - base
            picked[count] = r
            inside = jnp.logical_and(local >= 0, local < cells)
            count = count + inside.astype(jnp.int32)
        clear = pl.multiple_of(i * clear_rows, clear_rows)
        table[pl.ds(clear, clear_rows)] = jnp.zeros((clear_rows, lanes), jnp.float32)
        return count

    count = lax.fori_loop(0, receivers // group, scan, jnp.int32(0))
    lane_ids = lax.broadcasted_iota(jnp.int32, (steps, lanes), 1)
    together = 4

    def add(i, carry):
        todo = []
        for j in range(together):
            index = i * together + j
            r = picked[jnp.minimum(index, count - 1)]
            local = rec_ref[0, r] - base
            row = local // lanes
            lane = local % lanes
            start = pl.multiple_of((r // lanes) * lanes, lanes)
            traces = res_ref[0, :, pl.ds(start, lanes)]
            moved = pltpu.roll(traces, (lane - r) & (lanes - 1), axis=1)
            chosen = jnp.where(index < count, lane, -1)
            todo.append((row, jnp.where(lane_ids == chosen, SCALE * moved, 0.0)))
        for row, value in todo:
            for n in range(0, steps, 8):
                place = pl.ds(row + n * rows, 8, stride=rows)
                table[place, :] = table[place, :] + value[n : n + 8]
        return carry

    lax.fori_loop(0, (count + together - 1) // together, add, 0)


def receiver_table(rec_index, residual, depth, wide, lanes):
    steps = residual.shape[1]
    vmem = pl.BlockSpec(memory_space=pltpu.VMEM)
    rows = (depth + 2 * HALO) * wide
    return pl.pallas_call(
        functools.partial(table_kernel, HALO * wide),
        out_shape=jax.ShapeDtypeStruct((steps * rows, lanes), jnp.float32),
        in_specs=[pl.BlockSpec(memory_space=pltpu.SMEM), vmem],
        out_specs=vmem,
        scratch_shapes=[pltpu.SMEM((rec_index.shape[1],), jnp.int32)],
        compiler_params=pltpu.CompilerParams(vmem_limit_bytes=4 * 1024 * 1024),
    )(rec_index, residual)


def adjoint_kernel(
    groups, last_ref, prev_ref, vel_ref, gate_ref, src_ref, wave_ref, rec_ref, mx_ref, my_ref,
    grad_ref, adj_ref,
    u_even, l_even, u_odd, l_odd, coef, src_coef, vel_halo, image, first, second, part_sum,
    u_send, u_recv, l_send, l_recv, io_sem, start_send, start_recv, sum_send, sum_recv,
):
    depth, wide, lanes = last_ref.shape[1:]
    ring = 2 * HALO
    blocks = wave_ref.shape[0] // 2
    steps = 2 * blocks
    ext_rows = (depth + 2 * HALO) * wide
    n_x, n_hi = groups
    shot = lax.axis_index("shot")
    slab = lax.axis_index("slab")
    slabs = lax.axis_size("slab")
    x, hi = shot // n_hi, shot % n_hi
    has_down, has_up = slab > 0, slab < slabs - 1

    load_prev = pltpu.make_async_copy(prev_ref.at[0], u_even.at[0, pl.ds(ring, depth)], io_sem.at[0])
    load_last = pltpu.make_async_copy(last_ref.at[0], u_odd.at[pl.ds(HALO, depth)], io_sem.at[1])
    load_prev.start()
    load_last.start()

    empty = jnp.zeros((HALO, wide, lanes), jnp.float32)
    for z in range(0, depth + 2 * ring, HALO):
        l_even[0, z : z + HALO] = empty
        l_even[1, z : z + HALO] = empty
    for z in (0, HALO, depth + ring, depth + ring + HALO):
        u_even[0, z : z + HALO] = empty
        u_even[1, z : z + HALO] = empty
    for z in range(0, depth + 2 * HALO, HALO):
        l_odd[z : z + HALO] = empty
    for side, z in ((0, 0), (1, depth + HALO)):
        u_odd[z : z + HALO] = empty
        vel_halo[side] = empty

    barrier = pltpu.get_barrier_semaphore()
    peers = [(lax.rem(x + d, n_x) * n_hi + hi, slab) for d in range(1, n_x)]
    peers += [(x * n_hi + lax.rem(hi + d, n_hi), slab) for d in range(1, n_hi)]
    for peer in peers:
        pl.semaphore_signal(barrier, inc=1, device_id=peer, device_id_type=MESH)

    @pl.when(has_down)
    def _():
        pl.semaphore_signal(barrier, inc=1, device_id=(shot, slab - 1), device_id_type=MESH)

    @pl.when(has_up)
    def _():
        pl.semaphore_signal(barrier, inc=1, device_id=(shot, slab + 1), device_id_type=MESH)

    pl.semaphore_wait(barrier, len(peers) + has_down.astype(jnp.int32) + has_up.astype(jnp.int32))

    def remote(src, dst, send, recv, target):
        return pltpu.make_async_remote_copy(
            src_ref=src, dst_ref=dst, send_sem=send, recv_sem=recv,
            device_id=target, device_id_type=MESH,
        )

    def halo_copy(buf, send, recv, q, side, source=None):
        if side == 0:
            src, dst = buf.at[q, pl.ds(ring, ring)], buf.at[q, pl.ds(depth + ring, ring)]
        else:
            src, dst = buf.at[q, pl.ds(depth, ring)], buf.at[q, pl.ds(0, ring)]
        return remote(
            src if source is None else source, dst, send.at[q, side], recv.at[q, 1 - side],
            (shot, slab + (1 if side else -1)),
        )

    def start_copies(side):
        near = pl.ds(depth - HALO, HALO) if side else pl.ds(0, HALO)
        wider = pl.ds(depth - ring, ring) if side else pl.ds(0, ring)
        odd_place = pl.ds(0, HALO) if side else pl.ds(depth + HALO, HALO)
        target = (shot, slab + (1 if side else -1))
        return (
            remote(
                vel_ref.at[near], vel_halo.at[1 - side],
                start_send.at[0, side], start_recv.at[0, 1 - side], target,
            ),
            halo_copy(u_even, u_send, u_recv, 0, side, prev_ref.at[0, wider]),
            remote(
                last_ref.at[0, near], u_odd.at[odd_place],
                start_send.at[1, side], start_recv.at[1, 1 - side], target,
            ),
        )

    sides = ((0, has_down), (1, has_up))
    for side, has in sides:
        @pl.when(has)
        def _():
            for copy in start_copies(side):
                copy.start()

    ids = lax.broadcasted_iota(jnp.int32, (wide, lanes), 0) * lanes + lax.broadcasted_iota(
        jnp.int32, (wide, lanes), 1
    )
    source = src_ref[0] - slab * (depth * wide * lanes)

    def prepare(z, speed):
        speed = 0.4 * speed
        value = speed * speed
        coef[z + HALO] = value * (1.0 / SCALE)
        src_coef[z + HALO] = jnp.where(ids == source - z * (wide * lanes), value, 0.0)

    def prepare_own(z, carry):
        prepare(z, vel_ref[z])
        image[:, z] = jnp.zeros((wide // 8, 8, lanes), jnp.float32)
        return carry

    lax.fori_loop(0, depth, prepare_own, 0)
    load_prev.wait()
    load_last.wait()
    for side, has in sides:
        @pl.when(has)
        def _():
            velocity_in, _, last_in = start_copies(1 - side)
            velocity_in.wait_recv()
            last_in.wait_recv()

        for z in range(HALO):
            prepare(z + (depth if side else -HALO), vel_halo[side, z])

    def laplace(read, z):
        f = read(z)
        hi_part = f.astype(jnp.bfloat16)
        rest = f - hi_part.astype(jnp.float32)
        mid_part = rest.astype(jnp.bfloat16)
        lo_part = (rest - mid_part.astype(jnp.float32)).astype(jnp.bfloat16)
        total = CENTRE * f
        for k, weight in enumerate(WEIGHTS, 1):
            total = total + weight * (read(z + k) + read(z - k))
        total = total + jnp.dot(
            mx_ref[...],
            jnp.concatenate([hi_part, mid_part, lo_part], axis=0),
            preferred_element_type=jnp.float32,
        )
        total = total + jnp.dot(
            jnp.concatenate([hi_part, mid_part, lo_part], axis=1),
            my_ref[...],
            preferred_element_type=jnp.float32,
        )
        return f, total

    def update(even, odd, q, to_odd, is_l, wave, rec_start, layers):
        read_even = lambda z: even[q, z + ring]
        read_odd = lambda z: odd[z + HALO]
        for z in layers:
            f, lap = laplace(read_even if to_odd else read_odd, z)
            earlier = (read_odd if to_odd else read_even)(z)
            place = z + HALO
            if is_l:
                start = pl.multiple_of(rec_start + place * wide, 8)
                lap = lap + rec_ref[pl.ds(start, wide), :]
                if 0 <= z < depth:
                    now = u_even[q, z + ring] if to_odd else u_odd[place]
                    image[:, z] = image[:, z] + (now * lap).reshape(wide // 8, 8, lanes)
                fresh = 2.0 * f - earlier + coef[place] * lap
            else:
                fresh = 2.0 * f - earlier + coef[place] * lap + wave * src_coef[place]
            if to_odd:
                odd[place] = fresh
            else:
                even[1 - q, z + ring] = fresh

    def advance(b, q, even, odd, send, recv, is_l):
        waves = (wave_ref[2 * b], wave_ref[2 * b + 1])
        rec_starts = [(steps - 1 - (2 * b + i)) * ext_rows for i in range(2)]

        def layers(to_odd, some):
            i = 0 if to_odd else 1
            update(even, odd, q, to_odd, is_l, waves[i], rec_starts[i], some)

        more = b < blocks - 1
        can_recv = b >= 1 if is_l else b >= 0
        can_wait_send = b >= 2 if is_l else jnp.logical_and(b >= 1, more)
        half = depth // 2
        layers(True, range(HALO, depth - HALO))
        for side, has in sides:
            @pl.when(jnp.logical_and(has, can_recv))
            def _():
                halo_copy(even, send, recv, q, 1 - side).wait_recv()

            @pl.when(jnp.logical_and(has, can_wait_send))
            def _():
                halo_copy(even, send, recv, 1 - q, side).wait_send()

            first_half = side == 0
            layers(True, range(-HALO, HALO) if first_half else range(depth - HALO, depth + HALO))
            second_step = range(half) if first_half else range(half, depth)
            if is_l:
                layers(False, second_step)
            else:
                @pl.when(more)
                def _():
                    layers(False, second_step)

            @pl.when(jnp.logical_and(has, more))
            def _():
                halo_copy(even, send, recv, 1 - q, side).start()

    def block(b, carry):
        q = lax.rem(b, 2)
        advance(b, q, u_even, u_odd, u_send, u_recv, False)
        advance(b, q, l_even, l_odd, l_send, l_recv, True)
        return carry

    lax.fori_loop(0, blocks, block, 0)
    store = pltpu.make_async_copy(
        l_even.at[blocks % 2, pl.ds(ring, depth)], adj_ref.at[0], io_sem.at[0]
    )
    store.start()

    parts = 2
    rows = depth // parts

    def spread(c, d):
        target = lax.rem(x + d, n_x)
        return remote(
            image.at[pl.ds(target * n_hi, n_hi), pl.ds(c * rows, rows)], first.at[c, d - 1],
            sum_send.at[c, d - 1], sum_recv.at[c, d - 1], (target * n_hi + hi, slab),
        )

    def gather(c, d):
        target = lax.rem(hi + d, n_hi)
        return remote(
            part_sum.at[c, target], second.at[c, d - 1],
            sum_send.at[c, n_x - 2 + d], sum_recv.at[c, n_x - 2 + d], (x * n_hi + target, slab),
        )

    for c in range(parts):
        for p in range(wide // 8):
            gate = gate_ref[0, 8 * p : 8 * p + 8].astype(jnp.float32)
            image[p, c * rows : (c + 1) * rows] = image[p, c * rows : (c + 1) * rows] * gate
        for d in range(1, n_x):
            spread(c, d).start()
    for c in range(parts):
        for d in range(1, n_x):
            spread(c, d).wait_recv()
        for h in range(n_hi):
            total = image[x * n_hi + h, c * rows : (c + 1) * rows]
            for d in range(1, n_x):
                total = total + first[c, d - 1, h]
            part_sum[c, h] = total
        for d in range(1, n_hi):
            gather(c, d).start()
    for c in range(parts):
        for d in range(1, n_hi):
            gather(c, d).wait_recv()
        total = part_sum[c, hi]
        for d in range(1, n_hi):
            total = total + second[c, d - 1]
        speed = vel_ref[pl.ds(c * rows, rows), pl.ds(pl.multiple_of(shot * 8, 8), 8), :]
        grad_ref[pl.ds(c * rows, rows)] = (-0.32 / SCALE) * speed * total
    for c in range(parts):
        for d in range(1, n_x):
            spread(c, d).wait_send()
        for d in range(1, n_hi):
            gather(c, d).wait_send()
    store.wait()

    for side, has in sides:
        @pl.when(has)
        def _():
            velocity_out, _, last_out = start_copies(side)
            velocity_out.wait_send()
            last_out.wait_send()
            halo_copy(u_even, u_send, u_recv, blocks % 2, side).wait_send()
            halo_copy(u_even, u_send, u_recv, (blocks - 1) % 2, side).wait_send()
            halo_copy(l_even, l_send, l_recv, (blocks - 1) % 2, side).wait_send()


def on_device(groups, fwd_last, fwd_prev, velocity, aperture, rec_index, src_index, residual):
    depth, wide, lanes = fwd_last.shape[1:]
    steps = residual.shape[1]
    n_x, n_hi = groups
    table = receiver_table(rec_index, residual, depth, wide, lanes)
    waves = ricker((steps - 1 - jnp.arange(steps, dtype=jnp.int32)).astype(jnp.float32))
    mx = jnp.asarray(np.tile(band(wide), (1, 3)), jnp.bfloat16)
    my = jnp.asarray(np.tile(band(lanes), (3, 1)), jnp.bfloat16)
    hbm = pl.BlockSpec(memory_space=pl.ANY)
    vmem = pl.BlockSpec(memory_space=pltpu.VMEM)
    smem = pl.BlockSpec(memory_space=pltpu.SMEM)
    even = pltpu.VMEM((2, depth + 4 * HALO, wide, lanes), jnp.float32)
    odd = pltpu.VMEM((depth + 2 * HALO, wide, lanes), jnp.float32)
    pair = pltpu.SemaphoreType.DMA((2, 2))
    parts = 2
    return pl.pallas_call(
        functools.partial(adjoint_kernel, groups),
        out_shape=(
            jax.ShapeDtypeStruct((depth, 8, lanes), jnp.float32),
            jax.ShapeDtypeStruct(fwd_last.shape, jnp.float32),
        ),
        in_specs=[hbm, hbm, vmem, vmem, smem, smem, vmem, vmem, vmem],
        out_specs=(vmem, hbm),
        scratch_shapes=[
            even, even, odd, odd, odd, odd,
            pltpu.VMEM((2, HALO, wide, lanes), jnp.float32),
            pltpu.VMEM((wide // 8, depth, 8, lanes), jnp.float32),
            pltpu.VMEM((parts, n_x - 1, n_hi, depth // parts, 8, lanes), jnp.float32),
            pltpu.VMEM((parts, n_hi - 1, depth // parts, 8, lanes), jnp.float32),
            pltpu.VMEM((parts, n_hi, depth // parts, 8, lanes), jnp.float32),
            pair, pair, pair, pair,
            pltpu.SemaphoreType.DMA((2,)),
            pair, pair,
            pltpu.SemaphoreType.DMA((parts, n_x + n_hi - 2)),
            pltpu.SemaphoreType.DMA((parts, n_x + n_hi - 2)),
        ],
        compiler_params=pltpu.CompilerParams(
            collective_id=0, has_side_effects=True, vmem_limit_bytes=16 * 1024 * 1024
        ),
    )(fwd_last, fwd_prev, velocity, aperture, src_index, waves, table, mx, my)


def solution(mesh):
    in_specs = (
        P("shot", "slab", None, None),
        P("shot", "slab", None, None),
        P("slab", None, None),
        P("shot", None, None),
        P("shot", None),
        P("shot"),
        P("shot", None, None),
    )
    out_specs = (P("slab", "shot", None), P("shot", "slab", None, None))
    shots = mesh.shape["shot"]
    groups = (shots // 2, 2)
    return jax.shard_map(
        functools.partial(on_device, groups),
        mesh=mesh, in_specs=in_specs, out_specs=out_specs, check_vma=False,
    )
```

time: 226 us -> 155 us (0.69)
  Pallas kernels: 209 us -> 150 us
  local copies, waits for them, and re-layouts: 14.6 us -> 3.09 us
    pallas_call x1, Pallas kernels: 179 us -> 137 us  [on_device(): pl.pallas_call(functools.partial(adjoint_kernel, groups), out_shape=(jax....]
    pallas_call x1, Pallas kernels: 30.7 us -> 12.9 us  [receiver_table(): pl.pallas_call(functools.partial(table_kernel, HALO * wide), out_shape=ja...]
    unnamed x22 -> x18, local copies, waits for them, and re-layouts: 14.6 us -> 3.09 us
where the time goes in v2:
time: 155 us; the launch traced here: 154 us
  Pallas kernels  150 us (97%)
  local copies, waits for them, and re-layouts  3.09 us (2%)
    pallas_call x1, Pallas kernels, on_device(): pl.pallas_call(functools.partial(adjoint_kernel, groups), out_shape=(jax....  137 us
    pallas_call x1, Pallas kernels, receiver_table(): pl.pallas_call(functools.partial(table_kernel, HALO * wide), out_shape=ja...  12.9 us

profile of v2, /device:TPU:32, one launch (start us, length us, event | category | flops | bytes accessed | tf_op | source)
XLA Modules:
  0.0 154.5 jit_solution(12020190964611088192)
XLA Ops:
  0.6 0.0 copy-start.2
  0.6 0.0 copy-start.1
  0.7 0.0 copy-start
  1.4 0.0 copy-start.3
  1.4 0.9 copy-done.3
  2.4 0.0 copy-start.7
  2.4 0.7 copy-done.7
  3.1 0.0 copy-start.4
  3.1 0.0 copy-start.5
  3.1 0.0 copy-start.6
  3.1 12.9 %shard_map.104.rec_ref = f32[49152,128]{1,0:T(8,128)S(1)} custom-call(s32[1,2048]{1,0:T(1,128)S(1)} %copy-done.7, f32[1,32,2048]{2,1,0:T(8,128)S(1)} %copy-done.3), custom_call_target="tpu_custom_call" | custom-call | tf_op jit(solution)/shard_map/pallas_call | solution.py:80
  16.0 0.0 copy-done.2
  16.0 0.0 copy-done.1
  16.0 0.0 copy-done
  16.0 0.0 copy-done.4
  16.0 0.0 copy-done.5
  16.0 0.0 copy-done.6
  16.0 137.0 %shard_map.105 = (f32[16,8,128]{2,1,0:T(8,128)S(1)}, f32[1,16,64,128]{3,2,1,0:T(8,128)S(1)}) custom-call(f32[1,16,64,128]{3,2,1,0:T(8,128)S(1)} %copy-done, f32[1,16,64,128]{3,2,1,0:T(8,128)S(1)} %copy-done.1, f32[16,64,128]{2,1,0:T(8,128)S(1)} %copy-done.2, s32[1,64,128]{2,1,0:T(8,128)S(1)} %copy-done.5, s32[1]{0:T(128)S(6)} %copy.13.src_ref, ...), custom_call_target="tpu_custom_call" | custom-call | tf_op jit(solution)/shard_map/pallas_call | solution.py:375
  153.0 0.6 copy.14
  153.7 0.8 copy.15
  (1 shorter events, 0.0 us)
Async XLA Ops:
  0.6 15.4 %copy-start.2 = (f32[16,64,128]{2,1,0:T(8,128)S(1)}, f32[16,64,128]{2,1,0:T(8,128)}, u32[]{:S(2)}) copy-start(f32[16,64,128]{2,1,0:T(8,128)} %vel_ref.1) | copy-start | bytes 1572868
  0.6 15.4 %copy-start.1 = (f32[1,16,64,128]{3,2,1,0:T(8,128)S(1)}, f32[1,16,64,128]{3,2,1,0:T(8,128)}, u32[]{:S(2)}) copy-start(f32[1,16,64,128]{3,2,1,0:T(8,128)} %prev_ref.1) | copy-start | bytes 1572868
  0.7 15.4 %copy-start = (f32[1,16,64,128]{3,2,1,0:T(8,128)S(1)}, f32[1,16,64,128]{3,2,1,0:T(8,128)}, u32[]{:S(2)}) copy-start(f32[1,16,64,128]{3,2,1,0:T(8,128)} %last_ref.1) | copy-start | bytes 1572868
  1.4 1.0 copy-start.3
  2.4 0.7 copy-start.7
  3.1 12.9 %copy-start.4 = (bf16[384,128]{1,0:T(8,128)(2,1)S(1)}, bf16[384,128]{1,0:T(8,128)(2,1)}, u32[]{:S(2)}) copy-start(bf16[384,128]{1,0:T(8,128)(2,1)} %constant.17.clone.my_ref) | copy-start | bytes 294916
  3.1 12.9 %copy-start.5 = (s32[1,64,128]{2,1,0:T(8,128)S(1)}, s32[1,64,128]{2,1,0:T(8,128)}, u32[]{:S(2)}) copy-start(s32[1,64,128]{2,1,0:T(8,128)} %gate_ref.1) | copy-start | bytes 98308
  3.1 12.9 %copy-start.6 = (bf16[64,192]{1,0:T(8,128)(2,1)S(1)}, bf16[64,192]{1,0:T(8,128)(2,1)}, u32[]{:S(2)}) copy-start(bf16[64,192]{1,0:T(8,128)(2,1)} %constant.16.clone.mx_ref) | copy-start | bytes 73732

commit v3 on v2

--- a/solution.py
+++ b/solution.py
@@ -65,9 +65,10 @@
             chosen = jnp.where(index < count, lane, -1)
             todo.append((row, jnp.where(lane_ids == chosen, SCALE * moved, 0.0)))
         for row, value in todo:
-            for n in range(0, steps, 8):
-                place = pl.ds(row + n * rows, 8, stride=rows)
-                table[place, :] = table[place, :] + value[n : n + 8]
+            places = [pl.ds(row + n * rows, 8, stride=rows) for n in range(0, steps, 8)]
+            held = [table[place, :] for place in places]
+            for n, place in enumerate(places):
+                table[place, :] = held[n] + value[8 * n : 8 * n + 8]
         return carry
 
     lax.fori_loop(0, (count + together - 1) // together, add, 0)
@@ -145,19 +146,21 @@
             device_id=target, device_id_type=MESH,
         )
 
-    def halo_copy(buf, send, recv, q, side, source=None):
-        if side == 0:
-            src, dst = buf.at[q, pl.ds(ring, ring)], buf.at[q, pl.ds(depth + ring, ring)]
-        else:
-            src, dst = buf.at[q, pl.ds(depth, ring)], buf.at[q, pl.ds(0, ring)]
+    def halo_layers(side, half):
+        return depth - HALO * (half + 1) if side else HALO * half
+
+    def halo_copy(buf, send, recv, q, side, half, source=None):
+        start = halo_layers(side, half)
+        place = start - depth if side else start + depth
+        src = buf.at[q, pl.ds(ring + start, HALO)] if source is None else source
         return remote(
-            src if source is None else source, dst, send.at[q, side], recv.at[q, 1 - side],
-            (shot, slab + (1 if side else -1)),
+            src, buf.at[q, pl.ds(ring + place, HALO)],
+            send.at[q, side, half], recv.at[q, 1 - side, half], (shot, slab + (1 if side else -1)),
         )
 
     def start_copies(side):
-        near = pl.ds(depth - HALO, HALO) if side else pl.ds(0, HALO)
-        wider = pl.ds(depth - ring, ring) if side else pl.ds(0, ring)
+        near = pl.ds(halo_layers(side, 0), HALO)
+        far = pl.ds(halo_layers(side, 1), HALO)
         odd_place = pl.ds(0, HALO) if side else pl.ds(depth + HALO, HALO)
         target = (shot, slab + (1 if side else -1))
         return (
@@ -165,7 +168,8 @@
                 vel_ref.at[near], vel_halo.at[1 - side],
                 start_send.at[0, side], start_recv.at[0, 1 - side], target,
             ),
-            halo_copy(u_even, u_send, u_recv, 0, side, prev_ref.at[0, wider]),
+            halo_copy(u_even, u_send, u_recv, 0, side, 0, prev_ref.at[0, near]),
+            halo_copy(u_even, u_send, u_recv, 0, side, 1, prev_ref.at[0, far]),
             remote(
                 last_ref.at[0, near], u_odd.at[odd_place],
                 start_send.at[1, side], start_recv.at[1, 1 - side], target,
@@ -201,7 +205,7 @@
     for side, has in sides:
         @pl.when(has)
         def _():
-            velocity_in, _, last_in = start_copies(1 - side)
+            velocity_in, _, _, last_in = start_copies(1 - side)
             velocity_in.wait_recv()
             last_in.wait_recv()
 
@@ -250,49 +254,90 @@
             else:
                 even[1 - q, z + ring] = fresh
 
-    def advance(b, q, even, odd, send, recv, is_l):
-        waves = (wave_ref[2 * b], wave_ref[2 * b + 1])
-        rec_starts = [(steps - 1 - (2 * b + i)) * ext_rows for i in range(2)]
-
-        def layers(to_odd, some):
-            i = 0 if to_odd else 1
-            update(even, odd, q, to_odd, is_l, waves[i], rec_starts[i], some)
-
+    assert depth == 4 * HALO
+    fields = (
+        (u_even, u_odd, u_send, u_recv, False),
+        (l_even, l_odd, l_send, l_recv, True),
+    )
+
+    def layers(b, q, field, to_odd, some):
+        even, odd, _, _, is_l = field
+        i = 0 if to_odd else 1
+        step = 2 * b + i
+        rec_start = (steps - 1 - step) * ext_rows
+        update(even, odd, q, to_odd, is_l, wave_ref[step], rec_start, some)
+
+    def inner(b, q, field):
+        layers(b, q, field, True, range(HALO, depth - HALO))
+
+    def when(cond, run):
+        if cond is True:
+            run()
+        else:
+            pl.when(cond)(run)
+
+    def both(a, b):
+        return a if b is True else jnp.logical_and(a, b)
+
+    def arrive(q, field, side, half, some):
+        even, _, send, recv, _ = field
+        when(both(sides[side][1], some), halo_copy(even, send, recv, q, 1 - side, half).wait_recv)
+
+    def depart(b, q, field, side, half, sent_before, more):
+        even, _, send, recv, _ = field
+        has = sides[side][1]
+        start = halo_layers(side, half)
+
+        def second():
+            when(both(has, sent_before), halo_copy(even, send, recv, 1 - q, side, half).wait_send)
+            layers(b, q, field, False, range(start, start + HALO))
+
+        if field[4]:
+            second()
+        else:
+            when(more, second)
+        when(both(has, more), halo_copy(even, send, recv, 1 - q, side, half).start)
+
+    near_layers = (range(HALO), range(depth - HALO, depth))
+    far_layers = (range(-HALO, 0), range(depth, depth + HALO))
+
+    def near_first(i, field, side, half):
+        b, q = 2 * i, 0
+        arrive(q, field, side, half, i >= 1 if field[4] else True)
+        layers(b, q, field, True, far_layers[side] if half else near_layers[side])
+        depart(b, q, field, side, 1 - half, i >= 1, True)
+
+    def far_first(i, field, side):
+        b, q = 2 * i + 1, 1
         more = b < blocks - 1
-        can_recv = b >= 1 if is_l else b >= 0
-        can_wait_send = b >= 2 if is_l else jnp.logical_and(b >= 1, more)
-        half = depth // 2
-        layers(True, range(HALO, depth - HALO))
-        for side, has in sides:
-            @pl.when(jnp.logical_and(has, can_recv))
-            def _():
-                halo_copy(even, send, recv, q, 1 - side).wait_recv()
-
-            @pl.when(jnp.logical_and(has, can_wait_send))
-            def _():
-                halo_copy(even, send, recv, 1 - q, side).wait_send()
-
-            first_half = side == 0
-            layers(True, range(-HALO, HALO) if first_half else range(depth - HALO, depth + HALO))
-            second_step = range(half) if first_half else range(half, depth)
-            if is_l:
-                layers(False, second_step)
-            else:
-                @pl.when(more)
-                def _():
-                    layers(False, second_step)
-
-            @pl.when(jnp.logical_and(has, more))
-            def _():
-                halo_copy(even, send, recv, 1 - q, side).start()
-
-    def block(b, carry):
-        q = lax.rem(b, 2)
-        advance(b, q, u_even, u_odd, u_send, u_recv, False)
-        advance(b, q, l_even, l_odd, l_send, l_recv, True)
+        arrive(q, field, side, 1, True)
+        arrive(q, field, side, 0, True)
+        layers(b, q, field, True, near_layers[side])
+        layers(b, q, field, True, far_layers[side])
+        for half in range(2):
+            depart(b, q, field, side, half, i >= 1 if field[4] else True, more)
+
+    def two_blocks(i, carry):
+        u, l = fields
+        inner(2 * i, 0, u)
+        near_first(i, u, 0, 0)
+        near_first(i, u, 1, 0)
+        inner(2 * i, 0, l)
+        near_first(i, u, 0, 1)
+        near_first(i, u, 1, 1)
+        near_first(i, l, 0, 0)
+        near_first(i, l, 1, 0)
+        inner(2 * i + 1, 1, u)
+        near_first(i, l, 0, 1)
+        near_first(i, l, 1, 1)
+        far_first(i, u, 0)
+        far_first(i, u, 1)
+        inner(2 * i + 1, 1, l)
+        far_first(i, l, 0)
+        far_first(i, l, 1)
         return carry
 
-    lax.fori_loop(0, blocks, block, 0)
+    lax.fori_loop(0, blocks // 2, two_blocks, 0)
     store = pltpu.make_async_copy(
         l_even.at[blocks % 2, pl.ds(ring, depth)], adj_ref.at[0], io_sem.at[0]
     )
@@ -349,12 +394,13 @@
     for side, has in sides:
         @pl.when(has)
         def _():
-            velocity_out, _, last_out = start_copies(side)
+            velocity_out, _, _, last_out = start_copies(side)
             velocity_out.wait_send()
             last_out.wait_send()
-            halo_copy(u_even, u_send, u_recv, blocks % 2, side).wait_send()
-            halo_copy(u_even, u_send, u_recv, (blocks - 1) % 2, side).wait_send()
-            halo_copy(l_even, l_send, l_recv, (blocks - 1) % 2, side).wait_send()
+            for half in range(2):
+                halo_copy(u_even, u_send, u_recv, 0, side, half).wait_send()
+                halo_copy(u_even, u_send, u_recv, 1, side, half).wait_send()
+                halo_copy(l_even, l_send, l_recv, 1, side, half).wait_send()
 
 
 def on_device(groups, fwd_last, fwd_prev, velocity, aperture, rec_index, src_index, residual):
@@ -371,6 +417,7 @@
     even = pltpu.VMEM((2, depth + 4 * HALO, wide, lanes), jnp.float32)
     odd = pltpu.VMEM((depth + 2 * HALO, wide, lanes), jnp.float32)
     pair = pltpu.SemaphoreType.DMA((2, 2))
+    triple = pltpu.SemaphoreType.DMA((2, 2, 2))
     parts = 2
     return pl.pallas_call(
         functools.partial(adjoint_kernel, groups),
@@ -387,7 +434,7 @@
             pltpu.VMEM((parts, n_x - 1, n_hi, depth // parts, 8, lanes), jnp.float32),
             pltpu.VMEM((parts, n_hi - 1, depth // parts, 8, lanes), jnp.float32),
             pltpu.VMEM((parts, n_hi, depth // parts, 8, lanes), jnp.float32),
-            pair, pair, pair, pair,
+            triple, triple, triple, triple,
             pltpu.SemaphoreType.DMA((2,)),
             pair, pair,
             pltpu.SemaphoreType.DMA((parts, n_x + n_hi - 2)),

time: 155 us -> 145 us (0.935)
  Pallas kernels: 150 us -> 141 us
    pallas_call x1, Pallas kernels: 137 us -> 128 us  [on_device(): pl.pallas_call(functools.partial(adjoint_kernel, groups), out_shape=(jax....]
where the time goes in v3:
time: 145 us
  Pallas kernels  141 us (97%)
  local copies, waits for them, and re-layouts  3.09 us (2%)
  between operations  1.49 us (1%)
    pallas_call x1, Pallas kernels, on_device(): pl.pallas_call(functools.partial(adjoint_kernel, groups), out_shape=(jax....  128 us
    pallas_call x1, Pallas kernels, receiver_table(): pl.pallas_call(functools.partial(table_kernel, HALO * wide), out_shape=ja...  12.9 us
    unnamed x18, local copies, waits for them, and re-layouts  3.09 us

profile of v3, /device:TPU:32, one launch (start us, length us, event | category | flops | bytes accessed | tf_op | source)
XLA Modules:
  0.0 145.2 jit_solution(10880914990356318951)
XLA Ops:
  0.6 0.0 copy-start.2
  0.6 0.0 copy-start.1
  0.7 0.0 copy-start
  1.4 0.0 copy-start.3
  1.4 0.9 copy-done.3
  2.4 0.0 copy-start.7
  2.4 0.7 copy-done.7
  3.1 0.0 copy-start.4
  3.1 0.0 copy-start.5
  3.1 0.0 copy-start.6
  3.1 12.9 %shard_map.104.rec_ref = f32[49152,128]{1,0:T(8,128)S(1)} custom-call(s32[1,2048]{1,0:T(1,128)S(1)} %copy-done.7, f32[1,32,2048]{2,1,0:T(8,128)S(1)} %copy-done.3), custom_call_target="tpu_custom_call" | custom-call | tf_op jit(solution)/shard_map/pallas_call | solution.py:81
  16.0 0.0 copy-done.2
  16.0 0.0 copy-done.1
  16.0 0.0 copy-done
  16.0 0.0 copy-done.4
  16.0 0.0 copy-done.5
  16.0 0.0 copy-done.6
  16.0 127.7 %shard_map.105 = (f32[16,8,128]{2,1,0:T(8,128)S(1)}, f32[1,16,64,128]{3,2,1,0:T(8,128)S(1)}) custom-call(f32[1,16,64,128]{3,2,1,0:T(8,128)S(1)} %copy-done, f32[1,16,64,128]{3,2,1,0:T(8,128)S(1)} %copy-done.1, f32[16,64,128]{2,1,0:T(8,128)S(1)} %copy-done.2, s32[1,64,128]{2,1,0:T(8,128)S(1)} %copy-done.5, s32[1]{0:T(128)S(6)} %copy.13.src_ref, ...), custom_call_target="tpu_custom_call" | custom-call | tf_op jit(solution)/shard_map/pallas_call | solution.py:422
  143.8 0.6 copy.14
  144.4 0.8 copy.15
  (1 shorter events, 0.0 us)
Async XLA Ops:
  0.6 15.4 %copy-start.2 = (f32[16,64,128]{2,1,0:T(8,128)S(1)}, f32[16,64,128]{2,1,0:T(8,128)}, u32[]{:S(2)}) copy-start(f32[16,64,128]{2,1,0:T(8,128)} %vel_ref.1) | copy-start | bytes 1572868
  0.6 15.4 %copy-start.1 = (f32[1,16,64,128]{3,2,1,0:T(8,128)S(1)}, f32[1,16,64,128]{3,2,1,0:T(8,128)}, u32[]{:S(2)}) copy-start(f32[1,16,64,128]{3,2,1,0:T(8,128)} %prev_ref.1) | copy-start | bytes 1572868
  0.7 15.4 %copy-start = (f32[1,16,64,128]{3,2,1,0:T(8,128)S(1)}, f32[1,16,64,128]{3,2,1,0:T(8,128)}, u32[]{:S(2)}) copy-start(f32[1,16,64,128]{3,2,1,0:T(8,128)} %last_ref.1) | copy-start | bytes 1572868
  1.4 1.0 copy-start.3
  2.4 0.7 copy-start.7
  3.1 12.9 %copy-start.4 = (bf16[384,128]{1,0:T(8,128)(2,1)S(1)}, bf16[384,128]{1,0:T(8,128)(2,1)}, u32[]{:S(2)}) copy-start(bf16[384,128]{1,0:T(8,128)(2,1)} %constant.17.clone.my_ref) | copy-start | bytes 294916
  3.1 12.9 %copy-start.5 = (s32[1,64,128]{2,1,0:T(8,128)S(1)}, s32[1,64,128]{2,1,0:T(8,128)}, u32[]{:S(2)}) copy-start(s32[1,64,128]{2,1,0:T(8,128)} %gate_ref.1) | copy-start | bytes 98308
  3.1 12.9 %copy-start.6 = (bf16[64,192]{1,0:T(8,128)(2,1)S(1)}, bf16[64,192]{1,0:T(8,128)(2,1)}, u32[]{:S(2)}) copy-start(bf16[64,192]{1,0:T(8,128)(2,1)} %constant.16.clone.mx_ref) | copy-start | bytes 73732

commit v4 on v3

--- a/solution.py
+++ b/solution.py
@@ -31,9 +31,9 @@
     steps, receivers = res_ref.shape[1:]
     lanes = table.shape[1]
     rows = table.shape[0] // steps
-    cells = rows * lanes
     base = (lax.axis_index("slab") * (rows - 2 * first_row) - first_row) * lanes
-    group = 8
+    lane_bits = lanes.bit_length() - 1
+    group = 16
     clear_rows = rows * steps // (receivers // group)
 
     def scan(i, count):
@@ -41,7 +41,7 @@
             r = i * group + j
             local = rec_ref[0, r] - base
             picked[count] = r
-            inside = jnp.logical_and(local >= 0, local < cells)
+            inside = lax.shift_right_logical(local, lane_bits) < rows
             count = count + inside.astype(jnp.int32)
         clear = pl.multiple_of(i * clear_rows, clear_rows)
         table[pl.ds(clear, clear_rows)] = jnp.zeros((clear_rows, lanes), jnp.float32)
@@ -57,9 +57,9 @@
             index = i * together + j
             r = picked[jnp.minimum(index, count - 1)]
             local = rec_ref[0, r] - base
-            row = local // lanes
-            lane = local % lanes
-            start = pl.multiple_of((r // lanes) * lanes, lanes)
+            row = lax.shift_right_logical(local, lane_bits)
+            lane = local & (lanes - 1)
+            start = pl.multiple_of(r - (r & (lanes - 1)), lanes)
             traces = res_ref[0, :, pl.ds(start, lanes)]
             moved = pltpu.roll(traces, (lane - r) & (lanes - 1), axis=1)
             chosen = jnp.where(index < count, lane, -1)
@@ -85,14 +85,15 @@
         out_specs=vmem,
         scratch_shapes=[pltpu.SMEM((rec_index.shape[1],), jnp.int32)],
         compiler_params=pltpu.CompilerParams(vmem_limit_bytes=4 * 1024 * 1024),
+        cost_estimate=pl.CostEstimate(flops=0, bytes_accessed=4 * steps * rows * lanes, transcendentals=0),
     )(rec_index, residual)
 
 
 def adjoint_kernel(
-    groups, last_ref, prev_ref, vel_ref, gate_ref, src_ref, wave_ref, rec_ref, mx_ref, my_ref,
+    groups, last_ref, prev_ref, below_ref, above_ref, vel_ref, gate_ref, src_ref, wave_ref, rec_ref, mx_ref, my_ref,
     grad_ref, adj_ref,
     u_even, l_even, u_odd, l_odd, coef, src_coef, vel_halo, image, first, second, part_sum,
-    u_send, u_recv, l_send, l_recv, io_sem, start_send, start_recv, sum_send, sum_recv,
+    u_send, u_recv, l_send, l_recv, io_sem, edge_sem, sum_send, sum_recv,
 ):
     depth, wide, lanes = last_ref.shape[1:]
     ring = 2 * HALO
@@ -108,21 +109,27 @@
 
     load_prev = pltpu.make_async_copy(prev_ref.at[0], u_even.at[0, pl.ds(ring, depth)], io_sem.at[0])
     load_last = pltpu.make_async_copy(last_ref.at[0], u_odd.at[pl.ds(HALO, depth)], io_sem.at[1])
-    load_prev.start()
-    load_last.start()
+    loads = [load_prev, load_last]
+    for side, edge in ((0, below_ref), (1, above_ref)):
+        for i, (first_layer, count, place) in enumerate((
+            (0, ring, u_even.at[0, pl.ds(side * (depth + ring), ring)]),
+            (ring, HALO, u_odd.at[pl.ds(side * (depth + HALO), HALO)]),
+            (ring + HALO, HALO, vel_halo.at[side]),
+        )):
+            loads.append(
+                pltpu.make_async_copy(edge.at[pl.ds(first_layer, count)], place, edge_sem.at[side, i])
+            )
+    for load in loads:
+        load.start()
 
     empty = jnp.zeros((HALO, wide, lanes), jnp.float32)
     for z in range(0, depth + 2 * ring, HALO):
         l_even[0, z : z + HALO] = empty
         l_even[1, z : z + HALO] = empty
     for z in (0, HALO, depth + ring, depth + ring + HALO):
-        u_even[0, z : z + HALO] = empty
         u_even[1, z : z + HALO] = empty
     for z in range(0, depth + 2 * HALO, HALO):
         l_odd[z : z + HALO] = empty
-    for side, z in ((0, 0), (1, depth + HALO)):
-        u_odd[z : z + HALO] = empty
-        vel_halo[side] = empty
 
     barrier = pltpu.get_barrier_semaphore()
     peers = [(lax.rem(x + d, n_x) * n_hi + hi, slab) for d in range(1, n_x)]
@@ -149,39 +156,15 @@
     def halo_layers(side, half):
         return depth - HALO * (half + 1) if side else HALO * half
 
-    def halo_copy(buf, send, recv, q, side, half, source=None):
+    def halo_copy(buf, send, recv, q, side, half):
         start = halo_layers(side, half)
         place = start - depth if side else start + depth
-        src = buf.at[q, pl.ds(ring + start, HALO)] if source is None else source
         return remote(
-            src, buf.at[q, pl.ds(ring + place, HALO)],
+            buf.at[q, pl.ds(ring + start, HALO)], buf.at[q, pl.ds(ring + place, HALO)],
             send.at[q, side, half], recv.at[q, 1 - side, half], (shot, slab + (1 if side else -1)),
         )
 
-    def start_copies(side):
-        near = pl.ds(halo_layers(side, 0), HALO)
-        far = pl.ds(halo_layers(side, 1), HALO)
-        odd_place = pl.ds(0, HALO) if side else pl.ds(depth + HALO, HALO)
-        target = (shot, slab + (1 if side else -1))
-        return (
-            remote(
-                vel_ref.at[near], vel_halo.at[1 - side],
-                start_send.at[0, side], start_recv.at[0, 1 - side], target,
-            ),
-            halo_copy(u_even, u_send, u_recv, 0, side, 0, prev_ref.at[0, near]),
-            halo_copy(u_even, u_send, u_recv, 0, side, 1, prev_ref.at[0, far]),
-            remote(
-                last_ref.at[0, near], u_odd.at[odd_place],
-                start_send.at[1, side], start_recv.at[1, 1 - side], target,
-            ),
-        )
-
     sides = ((0, has_down), (1, has_up))
-    for side, has in sides:
-        @pl.when(has)
-        def _():
-            for copy in start_copies(side):
-                copy.start()
 
     ids = lax.broadcasted_iota(jnp.int32, (wide, lanes), 0) * lanes + lax.broadcasted_iota(
         jnp.int32, (wide, lanes), 1
@@ -200,15 +183,9 @@
         return carry
 
     lax.fori_loop(0, depth, prepare_own, 0)
-    load_prev.wait()
-    load_last.wait()
-    for side, has in sides:
-        @pl.when(has)
-        def _():
-            velocity_in, _, _, last_in = start_copies(1 - side)
-            velocity_in.wait_recv()
-            last_in.wait_recv()
-
+    for load in loads:
+        load.wait()
+    for side in range(2):
         for z in range(HALO):
             prepare(z + (depth if side else -HALO), vel_halo[side, z])
 
@@ -254,6 +231,30 @@
             else:
                 even[1 - q, z + ring] = fresh
 
+    parts = 2
+    rows = depth // parts
+
+    def spread(c, d):
+        target = lax.rem(x + d, n_x)
+        return remote(
+            image.at[pl.ds(target * n_hi, n_hi), pl.ds(c * rows, rows)], first.at[c, d - 1],
+            sum_send.at[c, d - 1], sum_recv.at[c, d - 1], (target * n_hi + hi, slab),
+        )
+
+    def gather(c, d):
+        target = lax.rem(hi + d, n_hi)
+        return remote(
+            part_sum.at[c, target], second.at[c, d - 1],
+            sum_send.at[c, n_x - 2 + d], sum_recv.at[c, n_x - 2 + d], (x * n_hi + target, slab),
+        )
+
+    def spread_part(c):
+        for p in range(wide // 8):
+            gate = gate_ref[0, 8 * p : 8 * p + 8].astype(jnp.float32)
+            image[p, c * rows : (c + 1) * rows] = image[p, c * rows : (c + 1) * rows] * gate
+        for d in range(1, n_x):
+            spread(c, d).start()
+
     assert depth == 4 * HALO
     fields = (
         (u_even, u_odd, u_send, u_recv, False),
@@ -303,7 +304,7 @@
 
     def near_first(i, field, side, half):
         b, q = 2 * i, 0
-        arrive(q, field, side, half, i >= 1 if field[4] else True)
+        arrive(q, field, side, half, i >= 1)
         layers(b, q, field, True, far_layers[side] if half else near_layers[side])
         depart(b, q, field, side, 1 - half, i >= 1, True)
 
@@ -315,7 +316,7 @@
         layers(b, q, field, True, near_layers[side])
         layers(b, q, field, True, far_layers[side])
         for half in range(2):
-            depart(b, q, field, side, half, i >= 1 if field[4] else True, more)
+            depart(b, q, field, side, half, i >= 1, more)
 
     def two_blocks(i, carry):
         u, l = fields
@@ -334,38 +335,21 @@
         far_first(i, u, 1)
         inner(2 * i + 1, 1, l)
         far_first(i, l, 0)
+
+        @pl.when(i == blocks // 2 - 1)
+        def _():
+            spread_part(0)
+
         far_first(i, l, 1)
         return carry
 
     lax.fori_loop(0, blocks // 2, two_blocks, 0)
+    spread_part(1)
     store = pltpu.make_async_copy(
         l_even.at[blocks % 2, pl.ds(ring, depth)], adj_ref.at[0], io_sem.at[0]
     )
     store.start()
 
-    parts = 2
-    rows = depth // parts
-
-    def spread(c, d):
-        target = lax.rem(x + d, n_x)
-        return remote(
-            image.at[pl.ds(target * n_hi, n_hi), pl.ds(c * rows, rows)], first.at[c, d - 1],
-            sum_send.at[c, d - 1], sum_recv.at[c, d - 1], (target * n_hi + hi, slab),
-        )
-
-    def gather(c, d):
-        target = lax.rem(hi + d, n_hi)
-        return remote(
-            part_sum.at[c, target], second.at[c, d - 1],
-            sum_send.at[c, n_x - 2 + d], sum_recv.at[c, n_x - 2 + d], (x * n_hi + target, slab),
-        )
-
-    for c in range(parts):
-        for p in range(wide // 8):
-            gate = gate_ref[0, 8 * p : 8 * p + 8].astype(jnp.float32)
-            image[p, c * rows : (c + 1) * rows] = image[p, c * rows : (c + 1) * rows] * gate
-        for d in range(1, n_x):
-            spread(c, d).start()
     for c in range(parts):
         for d in range(1, n_x):
             spread(c, d).wait_recv()
@@ -394,9 +378,6 @@
     for side, has in sides:
         @pl.when(has)
         def _():
-            velocity_out, _, _, last_out = start_copies(side)
-            velocity_out.wait_send()
-            last_out.wait_send()
             for half in range(2):
                 halo_copy(u_even, u_send, u_recv, 0, side, half).wait_send()
                 halo_copy(u_even, u_send, u_recv, 1, side, half).wait_send()
@@ -407,6 +388,12 @@
     depth, wide, lanes = fwd_last.shape[1:]
     steps = residual.shape[1]
     n_x, n_hi = groups
+    count = lax.axis_size("slab")
+    upward = [(i, i + 1) for i in range(count - 1)]
+    bottom = jnp.concatenate([fwd_prev[0, : 2 * HALO], fwd_last[0, :HALO], velocity[:HALO]])
+    top = jnp.concatenate([fwd_prev[0, -2 * HALO :], fwd_last[0, -HALO:], velocity[-HALO:]])
+    below = lax.ppermute(top, "slab", upward)
+    above = lax.ppermute(bottom, "slab", [(j, i) for i, j in upward])
     table = receiver_table(rec_index, residual, depth, wide, lanes)
     waves = ricker((steps - 1 - jnp.arange(steps, dtype=jnp.int32)).astype(jnp.float32))
     mx = jnp.asarray(np.tile(band(wide), (1, 3)), jnp.bfloat16)
@@ -416,7 +403,6 @@
     smem = pl.BlockSpec(memory_space=pltpu.SMEM)
     even = pltpu.VMEM((2, depth + 4 * HALO, wide, lanes), jnp.float32)
     odd = pltpu.VMEM((depth + 2 * HALO, wide, lanes), jnp.float32)
-    pair = pltpu.SemaphoreType.DMA((2, 2))
     triple = pltpu.SemaphoreType.DMA((2, 2, 2))
     parts = 2
     return pl.pallas_call(
@@ -425,7 +411,7 @@
             jax.ShapeDtypeStruct((depth, 8, lanes), jnp.float32),
             jax.ShapeDtypeStruct(fwd_last.shape, jnp.float32),
         ),
-        in_specs=[hbm, hbm, vmem, vmem, smem, smem, vmem, vmem, vmem],
+        in_specs=[hbm, hbm, hbm, hbm, vmem, vmem, smem, smem, vmem, vmem, vmem],
         out_specs=(vmem, hbm),
         scratch_shapes=[
             even, even, odd, odd, odd, odd,
@@ -436,14 +422,14 @@
             pltpu.VMEM((parts, n_hi, depth // parts, 8, lanes), jnp.float32),
             triple, triple, triple, triple,
             pltpu.SemaphoreType.DMA((2,)),
-            pair, pair,
+            pltpu.SemaphoreType.DMA((2, 3)),
             pltpu.SemaphoreType.DMA((parts, n_x + n_hi - 2)),
             pltpu.SemaphoreType.DMA((parts, n_x + n_hi - 2)),
         ],
         compiler_params=pltpu.CompilerParams(
             collective_id=0, has_side_effects=True, vmem_limit_bytes=16 * 1024 * 1024
         ),
-    )(fwd_last, fwd_prev, velocity, aperture, src_index, waves, table, mx, my)
+    )(fwd_last, fwd_prev, below, above, velocity, aperture, src_index, waves, table, mx, my)
 
 
 def solution(mesh):

time: 145 us -> 145 us (level)
  Pallas kernels: 141 us -> 130 us
  starting transfers between devices: 0 us -> 7.67 us
  local copies, waits for them, and re-layouts: 3.09 us -> 6.27 us
    pallas_call x1, Pallas kernels: 128 us -> 117 us  [on_device(): pl.pallas_call(functools.partial(adjoint_kernel, groups), out_shape=(jax....]
    ppermute x0 -> x2, starting transfers between devices: none -> 7.67 us  [the longest x1 5.75 us: on_device(): above = lax.ppermute(bottom, 'slab', [(j, i) for i, j in upward])]
    squeeze x0 -> x2, local copies, waits for them, and re-layouts: none -> 2.18 us  [the longest x1 1.11 us: on_device(): fwd_last[0, :HALO]]
  transfers between devices with their start and end apart: 0 -> 2, of which waited for: 0 -> 0; matrix products, arithmetic and copies ran while one was open for 0% -> 0% of each run, Pallas kernels for 0% -> 8%
where the time goes in v4:
time: 145 us
  Pallas kernels  130 us (90%)
  starting transfers between devices  7.67 us (5%)
  local copies, waits for them, and re-layouts  6.27 us (4%)
  between operations  1.46 us (1%)
    pallas_call x1, Pallas kernels, on_device(): pl.pallas_call(functools.partial(adjoint_kernel, groups), out_shape=(jax....  117 us
    pallas_call x1, Pallas kernels, receiver_table(): pl.pallas_call(functools.partial(table_kernel, HALO * wide), out_shape=ja...  12.2 us
    ppermute x1, starting transfers between devices, on_device(): above = lax.ppermute(bottom, 'slab', [(j, i) for i, j in upward])  5.75 us
    unnamed x18, local copies, waits for them, and re-layouts  3.1 us
  transfers between devices with their start and end apart: 2, of which 0 were waited for; matrix products, arithmetic and copies ran while one was open for 0% of the time, Pallas kernels for 8%

profile of v4, /device:TPU:32, one launch (start us, length us, event | category | flops | bytes accessed | tf_op | source)
XLA Modules:
  0.0 145.1 jit_solution(14297118879188572010)
XLA Ops:
  0.6 0.0 copy-start.4
  0.6 0.0 copy-start.6
  0.7 0.0 copy-start.1
  0.7 0.0 copy-start.2
  0.7 0.0 copy-start
  0.7 0.0 copy-start.5
  0.7 1.1 slice_bitcast_fusion.2
  1.8 1.0 fusion
  2.8 1.1 slice_bitcast_fusion
  3.9 1.9 %collective-permute-start = (f32[16,64,128]{2,1,0:T(8,128)S(1)}, f32[16,64,128]{2,1,0:T(8,128)S(1)}, u32[]{:S(2)}, u32[]{:S(2)}) collective-permute-start(f32[16,64,128]{2,1,0:T(8,128)S(1)} %pad_maximum_fusion), channel_id=1, source_target_pairs={{0,1},{1,2},{2,3},{3,4},{4,5},{5,6},{6,7},{7,8},{8,9},{9,10},{10,1... | collective-permute-start | bytes 1572872 | tf_op jit(solution)/shard_map/ppermute | solution.py:395
  5.9 5.8 %collective-permute-start.1 = (f32[16,64,128]{2,1,0:T(8,128)S(1)}, f32[16,64,128]{2,1,0:T(8,128)S(1)}, u32[]{:S(2)}, u32[]{:S(2)}) collective-permute-start(f32[16,64,128]{2,1,0:T(8,128)S(1)} %pad_maximum_fusion.1), channel_id=1, source_target_pairs={{1,0},{2,1},{3,2},{4,3},{5,4},{6,5},{7,6},{8,7},{9,8},{10,9},{11,1... | collective-permute-start | bytes 1572872 | tf_op jit(solution)/shard_map/ppermute | solution.py:396
  12.3 0.0 copy-start.3
  12.3 0.9 copy-done.3
  13.3 0.0 copy-start.7
  13.3 0.7 copy-done.7
  14.0 12.2 %shard_map.104.rec_ref = f32[49152,128]{1,0:T(8,128)S(1)} custom-call(s32[1,2048]{1,0:T(1,128)S(1)} %copy-done.7, f32[1,32,2048]{2,1,0:T(8,128)S(1)} %copy-done.3), custom_call_target="tpu_custom_call" | custom-call | bytes 25165824 | tf_op jit(solution)/shard_map/pallas_call | solution.py:81
  26.2 0.0 collective-permute-done.below_ref
  26.2 0.0 collective-permute-done.1.above_ref
  26.2 0.0 copy-done.4
  26.3 0.0 copy-done.6
  26.3 0.0 copy-done.1
  26.3 0.0 copy-done.2
  26.3 0.0 copy-done
  26.3 0.0 copy-done.5
  26.3 117.3 %shard_map.105 = (f32[16,8,128]{2,1,0:T(8,128)S(1)}, f32[1,16,64,128]{3,2,1,0:T(8,128)S(1)}) custom-call(f32[1,16,64,128]{3,2,1,0:T(8,128)S(1)} %copy-done.1, f32[1,16,64,128]{3,2,1,0:T(8,128)S(1)} %copy-done, f32[16,64,128]{2,1,0:T(8,128)S(1)} %collective-permute-done.below_ref, f32[16,64,128]{2,1,0:T(8,128)S(1)} %collective-permute-done.1.above_ref, ...), custom_call_target="tpu_custom_call" | custom-call | tf_op jit(solution)/shard_map/pallas_call | solution.py:408
  143.6 0.6 copy.14
  144.3 0.8 copy.15
  (3 shorter events, 0.1 us)
Async XLA Ops:
  0.6 25.6 %copy-start.4 = (bf16[384,128]{1,0:T(8,128)(2,1)S(1)}, bf16[384,128]{1,0:T(8,128)(2,1)}, u32[]{:S(2)}) copy-start(bf16[384,128]{1,0:T(8,128)(2,1)} %constant.17.clone.my_ref) | copy-start | bytes 294916
  0.6 25.6 %copy-start.6 = (bf16[64,192]{1,0:T(8,128)(2,1)S(1)}, bf16[64,192]{1,0:T(8,128)(2,1)}, u32[]{:S(2)}) copy-start(bf16[64,192]{1,0:T(8,128)(2,1)} %constant.16.clone.mx_ref) | copy-start | bytes 73732
  0.7 25.6 %copy-start.1 = (f32[1,16,64,128]{3,2,1,0:T(8,128)S(1)}, f32[1,16,64,128]{3,2,1,0:T(8,128)}, u32[]{:S(2)}) copy-start(f32[1,16,64,128]{3,2,1,0:T(8,128)} %last_ref.1) | copy-start | bytes 1572868
  0.7 25.6 %copy-start.2 = (f32[16,64,128]{2,1,0:T(8,128)S(1)}, f32[16,64,128]{2,1,0:T(8,128)}, u32[]{:S(2)}) copy-start(f32[16,64,128]{2,1,0:T(8,128)} %vel_ref.1) | copy-start | bytes 1572868
  0.7 25.6 %copy-start = (f32[1,16,64,128]{3,2,1,0:T(8,128)S(1)}, f32[1,16,64,128]{3,2,1,0:T(8,128)}, u32[]{:S(2)}) copy-start(f32[1,16,64,128]{3,2,1,0:T(8,128)} %prev_ref.1) | copy-start | bytes 1572868
  0.7 25.6 %copy-start.5 = (s32[1,64,128]{2,1,0:T(8,128)S(1)}, s32[1,64,128]{2,1,0:T(8,128)}, u32[]{:S(2)}) copy-start(s32[1,64,128]{2,1,0:T(8,128)} %gate_ref.1) | copy-start | bytes 98308
  3.9 22.3 %collective-permute-start = (f32[16,64,128]{2,1,0:T(8,128)S(1)}, f32[16,64,128]{2,1,0:T(8,128)S(1)}, u32[]{:S(2)}, u32[]{:S(2)}) collective-permute-start(f32[16,64,128]{2,1,0:T(8,128)S(1)} %pad_maximum_fusion), channel_id=1, source_target_pairs={{0,1},{1,2},{2,3},{3,4},{4,5},{5,6},{6,7},{7,8},{8,9},{9,10},{10,1... | collective-permute-start | bytes 1572872 | tf_op jit(solution)/shard_map/ppermute | solution.py:395
  5.9 20.3 %collective-permute-start.1 = (f32[16,64,128]{2,1,0:T(8,128)S(1)}, f32[16,64,128]{2,1,0:T(8,128)S(1)}, u32[]{:S(2)}, u32[]{:S(2)}) collective-permute-start(f32[16,64,128]{2,1,0:T(8,128)S(1)} %pad_maximum_fusion.1), channel_id=1, source_target_pairs={{1,0},{2,1},{3,2},{4,3},{5,4},{6,5},{7,6},{8,7},{9,8},{10,9},{11,1... | collective-permute-start | bytes 1572872 | tf_op jit(solution)/shard_map/ppermute | solution.py:396
  12.3 1.0 copy-start.3
  13.3 0.7 copy-start.7

commit v5 on v3

--- a/solution.py
+++ b/solution.py
@@ -31,9 +31,9 @@
     steps, receivers = res_ref.shape[1:]
     lanes = table.shape[1]
     rows = table.shape[0] // steps
-    cells = rows * lanes
     base = (lax.axis_index("slab") * (rows - 2 * first_row) - first_row) * lanes
-    group = 8
+    lane_bits = lanes.bit_length() - 1
+    group = 16
     clear_rows = rows * steps // (receivers // group)
 
     def scan(i, count):
@@ -41,7 +41,7 @@
             r = i * group + j
             local = rec_ref[0, r] - base
             picked[count] = r
-            inside = jnp.logical_and(local >= 0, local < cells)
+            inside = lax.shift_right_logical(local, lane_bits) < rows
             count = count + inside.astype(jnp.int32)
         clear = pl.multiple_of(i * clear_rows, clear_rows)
         table[pl.ds(clear, clear_rows)] = jnp.zeros((clear_rows, lanes), jnp.float32)
@@ -57,9 +57,9 @@
             index = i * together + j
             r = picked[jnp.minimum(index, count - 1)]
             local = rec_ref[0, r] - base
-            row = local // lanes
-            lane = local % lanes
-            start = pl.multiple_of((r // lanes) * lanes, lanes)
+            row = lax.shift_right_logical(local, lane_bits)
+            lane = local & (lanes - 1)
+            start = pl.multiple_of(r - (r & (lanes - 1)), lanes)
             traces = res_ref[0, :, pl.ds(start, lanes)]
             moved = pltpu.roll(traces, (lane - r) & (lanes - 1), axis=1)
             chosen = jnp.where(index < count, lane, -1)
@@ -85,6 +85,7 @@
         out_specs=vmem,
         scratch_shapes=[pltpu.SMEM((rec_index.shape[1],), jnp.int32)],
         compiler_params=pltpu.CompilerParams(vmem_limit_bytes=4 * 1024 * 1024),
+        cost_estimate=pl.CostEstimate(flops=0, bytes_accessed=4 * steps * rows * lanes, transcendentals=0),
     )(rec_index, residual)
 
 
@@ -180,7 +181,8 @@
     for side, has in sides:
         @pl.when(has)
         def _():
-            for copy in start_copies(side):
+            velocity_out, near_out, far_out, last_out = start_copies(side)
+            for copy in (near_out, far_out, last_out, velocity_out):
                 copy.start()
 
     ids = lax.broadcasted_iota(jnp.int32, (wide, lanes), 0) * lanes + lax.broadcasted_iota(
@@ -202,15 +204,16 @@
     lax.fori_loop(0, depth, prepare_own, 0)
     load_prev.wait()
     load_last.wait()
-    for side, has in sides:
-        @pl.when(has)
-        def _():
-            velocity_in, _, _, last_in = start_copies(1 - side)
-            velocity_in.wait_recv()
-            last_in.wait_recv()
-
-        for z in range(HALO):
-            prepare(z + (depth if side else -HALO), vel_halo[side, z])
+    def first_halo():
+        for side, has in sides:
+            @pl.when(has)
+            def _():
+                velocity_in, _, _, last_in = start_copies(1 - side)
+                last_in.wait_recv()
+                velocity_in.wait_recv()
+
+            for z in range(HALO):
+                prepare(z + (depth if side else -HALO), vel_halo[side, z])
 
     def laplace(read, z):
         f = read(z)
@@ -254,6 +257,30 @@
             else:
                 even[1 - q, z + ring] = fresh
 
+    parts = 2
+    rows = depth // parts
+
+    def spread(c, d):
+        target = lax.rem(x + d, n_x)
+        return remote(
+            image.at[pl.ds(target * n_hi, n_hi), pl.ds(c * rows, rows)], first.at[c, d - 1],
+            sum_send.at[c, d - 1], sum_recv.at[c, d - 1], (target * n_hi + hi, slab),
+        )
+
+    def gather(c, d):
+        target = lax.rem(hi + d, n_hi)
+        return remote(
+            part_sum.at[c, target], second.at[c, d - 1],
+            sum_send.at[c, n_x - 2 + d], sum_recv.at[c, n_x - 2 + d], (x * n_hi + target, slab),
+        )
+
+    def spread_part(c):
+        for p in range(wide // 8):
+            gate = gate_ref[0, 8 * p : 8 * p + 8].astype(jnp.float32)
+            image[p, c * rows : (c + 1) * rows] = image[p, c * rows : (c + 1) * rows] * gate
+        for d in range(1, n_x):
+            spread(c, d).start()
+
     assert depth == 4 * HALO
     fields = (
         (u_even, u_odd, u_send, u_recv, False),
@@ -323,6 +350,7 @@
         near_first(i, u, 0, 0)
         near_first(i, u, 1, 0)
         inner(2 * i, 0, l)
+        pl.when(i == 0)(first_halo)
         near_first(i, u, 0, 1)
         near_first(i, u, 1, 1)
         near_first(i, l, 0, 0)
@@ -334,38 +362,21 @@
         far_first(i, u, 1)
         inner(2 * i + 1, 1, l)
         far_first(i, l, 0)
+
+        @pl.when(i == blocks // 2 - 1)
+        def _():
+            spread_part(0)
+
         far_first(i, l, 1)
         return carry
 
     lax.fori_loop(0, blocks // 2, two_blocks, 0)
+    spread_part(1)
     store = pltpu.make_async_copy(
         l_even.at[blocks % 2, pl.ds(ring, depth)], adj_ref.at[0], io_sem.at[0]
     )
     store.start()
 
-    parts = 2
-    rows = depth // parts
-
-    def spread(c, d):
-        target = lax.rem(x + d, n_x)
-        return remote(
-            image.at[pl.ds(target * n_hi, n_hi), pl.ds(c * rows, rows)], first.at[c, d - 1],
-            sum_send.at[c, d - 1], sum_recv.at[c, d - 1], (target * n_hi + hi, slab),
-        )
-
-    def gather(c, d):
-        target = lax.rem(hi + d, n_hi)
-        return remote(
-            part_sum.at[c, target], second.at[c, d - 1],
-            sum_send.at[c, n_x - 2 + d], sum_recv.at[c, n_x - 2 + d], (x * n_hi + target, slab),
-        )
-
-    for c in range(parts):
-        for p in range(wide // 8):
-            gate = gate_ref[0, 8 * p : 8 * p + 8].astype(jnp.float32)
-            image[p, c * rows : (c + 1) * rows] = image[p, c * rows : (c + 1) * rows] * gate
-        for d in range(1, n_x):
-            spread(c, d).start()
     for c in range(parts):
         for d in range(1, n_x):
             spread(c, d).wait_recv()

time: 145 us -> 141 us (0.972)
  Pallas kernels: 141 us -> 136 us
    pallas_call x1, Pallas kernels: 128 us -> 124 us  [on_device(): pl.pallas_call(functools.partial(adjoint_kernel, groups), out_shape=(jax....]
where the time goes in v5:
time: 141 us
  Pallas kernels  136 us (96%)
  local copies, waits for them, and re-layouts  3.09 us (2%)
  between operations  1.49 us (1%)
    pallas_call x1, Pallas kernels, on_device(): pl.pallas_call(functools.partial(adjoint_kernel, groups), out_shape=(jax....  124 us
    pallas_call x1, Pallas kernels, receiver_table(): pl.pallas_call(functools.partial(table_kernel, HALO * wide), out_shape=ja...  12.1 us
    unnamed x18, local copies, waits for them, and re-layouts  3.09 us

profile of v5, /device:TPU:32, one launch (start us, length us, event | category | flops | bytes accessed | tf_op | source)
XLA Modules:
  0.0 141.0 jit_solution(6909786054488454533)
XLA Ops:
  0.6 0.0 copy-start.2
  0.6 0.0 copy-start.1
  0.7 0.0 copy-start
  1.4 0.0 copy-start.3
  1.4 0.9 copy-done.3
  2.4 0.0 copy-start.7
  2.4 0.7 copy-done.7
  3.1 0.0 copy-start.4
  3.1 0.0 copy-start.5
  3.1 0.0 copy-start.6
  3.1 12.1 %shard_map.104.rec_ref = f32[49152,128]{1,0:T(8,128)S(1)} custom-call(s32[1,2048]{1,0:T(1,128)S(1)} %copy-done.7, f32[1,32,2048]{2,1,0:T(8,128)S(1)} %copy-done.3), custom_call_target="tpu_custom_call" | custom-call | bytes 25165824 | tf_op jit(solution)/shard_map/pallas_call | solution.py:81
  15.2 0.0 copy-done.2
  15.2 0.0 copy-done.1
  15.2 0.0 copy-done
  15.2 0.0 copy-done.4
  15.2 0.0 copy-done.5
  15.2 0.0 copy-done.6
  15.2 124.3 %shard_map.105 = (f32[16,8,128]{2,1,0:T(8,128)S(1)}, f32[1,16,64,128]{3,2,1,0:T(8,128)S(1)}) custom-call(f32[1,16,64,128]{3,2,1,0:T(8,128)S(1)} %copy-done, f32[1,16,64,128]{3,2,1,0:T(8,128)S(1)} %copy-done.1, f32[16,64,128]{2,1,0:T(8,128)S(1)} %copy-done.2, s32[1,64,128]{2,1,0:T(8,128)S(1)} %copy-done.5, s32[1]{0:T(128)S(6)} %copy.13.src_ref, ...), custom_call_target="tpu_custom_call" | custom-call | tf_op jit(solution)/shard_map/pallas_call | solution.py:433
  139.5 0.6 copy.14
  140.2 0.8 copy.15
  (1 shorter events, 0.0 us)
Async XLA Ops:
  0.6 14.5 %copy-start.2 = (f32[16,64,128]{2,1,0:T(8,128)S(1)}, f32[16,64,128]{2,1,0:T(8,128)}, u32[]{:S(2)}) copy-start(f32[16,64,128]{2,1,0:T(8,128)} %vel_ref.1) | copy-start | bytes 1572868
  0.6 14.5 %copy-start.1 = (f32[1,16,64,128]{3,2,1,0:T(8,128)S(1)}, f32[1,16,64,128]{3,2,1,0:T(8,128)}, u32[]{:S(2)}) copy-start(f32[1,16,64,128]{3,2,1,0:T(8,128)} %prev_ref.1) | copy-start | bytes 1572868
  0.7 14.5 %copy-start = (f32[1,16,64,128]{3,2,1,0:T(8,128)S(1)}, f32[1,16,64,128]{3,2,1,0:T(8,128)}, u32[]{:S(2)}) copy-start(f32[1,16,64,128]{3,2,1,0:T(8,128)} %last_ref.1) | copy-start | bytes 1572868
  1.4 1.0 copy-start.3
  2.4 0.7 copy-start.7
  3.1 12.1 %copy-start.4 = (bf16[384,128]{1,0:T(8,128)(2,1)S(1)}, bf16[384,128]{1,0:T(8,128)(2,1)}, u32[]{:S(2)}) copy-start(bf16[384,128]{1,0:T(8,128)(2,1)} %constant.17.clone.my_ref) | copy-start | bytes 294916
  3.1 12.1 %copy-start.5 = (s32[1,64,128]{2,1,0:T(8,128)S(1)}, s32[1,64,128]{2,1,0:T(8,128)}, u32[]{:S(2)}) copy-start(s32[1,64,128]{2,1,0:T(8,128)} %gate_ref.1) | copy-start | bytes 98308
  3.1 12.1 %copy-start.6 = (bf16[64,192]{1,0:T(8,128)(2,1)S(1)}, bf16[64,192]{1,0:T(8,128)(2,1)}, u32[]{:S(2)}) copy-start(bf16[64,192]{1,0:T(8,128)(2,1)} %constant.16.clone.mx_ref) | copy-start | bytes 73732
